TPU v7x, 32 devices: a whole 2x2x4 slice. The times are simulated.
32 devices in a mesh: gx: 4 (over z), gy: 8 (over y, x, core).
Axes of the slice: x: 2, y: 2, z: 4, core: 2. Of those that a mesh axis runs over, the one named last changes fastest.
Arguments:
- positions: float32 [3, 524288], P(None, ('gx', 'gy')), may hold values from -0.5 to 0.5, as said below
- charges: float32 [524288], P(('gx', 'gy')), may hold values from -0.36 to 0.36
- near_leaves: int32 [4096, 27], P(('gx', 'gy')), may hold values from -1 to 4095, as said below
- near_offsets: int32 [4096, 27], P(('gx', 'gy')), may hold values from 0 to 26, as said below
- far_leaves: int32 [4096, 189], P(('gx', 'gy')), may hold values from -1 to 639, as said below
- far_leaf_class: int32 [4096, 189], P(('gx', 'gy')), may hold values from 0 to 15
- leaf_plan: int32 [32, 32, 16], P(('gx', 'gy')), may hold values from -1 to 127, as said below
- far_parents: int32 [512, 189], P(('gx', 'gy')), may hold values from -1 to 143, as said below
- far_parent_class: int32 [512, 189], P(('gx', 'gy')), may hold values from 0 to 15
- parent_plan: int32 [32, 32, 4], P(('gx', 'gy')), may hold values from -1 to 15, as said below
- coarse_lists: int32 [8, 7], replicated, may hold values from 0 to 7, as said below
- coarse_class: int32 [8, 7], replicated, may hold values from 0 to 15
- up_shift: float32 [8, 286, 286], replicated, may hold values from -4 to 4
- down_shift: float32 [8, 286, 286], replicated, may hold values from -4 to 4
- far_shift: float32 [16, 286, 286], replicated, may hold values from -2 to 2
Outputs:
- potential: float32 [524288], P(('gx', 'gy'))
Inputs may be any that keep to these rules, and one draw needn't show every extreme that they name: `positions`: each coordinate lies within half a leaf width of its leaf centre. `near_leaves`: entry 0 of every list is the leaf itself with offset class 13; the other entries name leaves at most 32 before the first leaf or after the last leaf of the list's own device; -1 pads a list's tail. `near_offsets`: entry 0 is 13. `leaf_plan`: row d, column o lists distinct local indices of leaves of device o that device d names, then -1; at most 16 a pair, reached in every draw; a device names none of its own. `far_leaves`: slots name only own leaves or filled entries of the device's row of leaf_plan; -1 pads a list's tail. `parent_plan`: as leaf_plan, for parent cells, at most 4 a pair, reached in every draw. `far_parents`: slots name only own parents or filled entries of the device's row of parent_plan; -1 pads a list's tail. `coarse_lists`: each row names distinct cells other than its own.
All inputs are finite; a program needn't handle non-finite values.
Results may differ from a plain program's by a relative error of at most 0.0003.
Values sent between devices are 32-bit elements; how exact they have to be, the bound alone decides.
A program may use at most 192 MiB of HBM per device.

v0:
```python
import jax
import jax.numpy as jnp
import numpy as np
from jax import lax
from jax.sharding import PartitionSpec as P

ORDER = 10
RIM = 32


softening = 0.05
highest = lax.Precision.HIGHEST


def extended_2(x, sides, width):
    for axis, dim in sides:
        size, length = (lax.axis_size(axis), x.shape[dim])
        up = [(i, (i + 1) % size) for i in range(size - 1)]
        down = [(j, i) for i, j in up]
        last = lax.slice_in_dim(x, length - width, length, axis=dim)
        first = lax.slice_in_dim(x, 0, width, axis=dim)
        before = lax.ppermute(last, axis, up)
        after = lax.ppermute(first, axis, down)
        x = jnp.concatenate([before, x, after], axis=dim)
    return x


def exponents(order):
    entries = []
    for degree in range(order + 1):
        for first_power in range(degree, -1, -1):
            for second_power in range(degree - first_power, -1, -1):
                entries.append((first_power, second_power, degree - first_power - second_power))
    return np.array(entries, dtype=np.int32).T


def basis(coords):
    scaled = 2.0 * coords
    powers = [jnp.ones_like(scaled)]
    for degree in range(ORDER):
        powers.append(powers[-1] * scaled)
    stacked = jnp.stack(powers)
    exponent_table = exponents(ORDER)
    return (
        stacked[exponent_table[0], 0]
        * stacked[exponent_table[1], 1]
        * stacked[exponent_table[2], 2]
    )


def upward(children, up_shift):
    grouped = children.reshape(children.shape[0], -1, 8)
    return jnp.einsum("cab,bnc->an", up_shift, grouped, precision=highest)


def downward(parents, down_shift):
    spread = jnp.einsum("cab,bn->anc", down_shift, parents, precision=highest)
    return spread.reshape(spread.shape[0], -1)


def far_field(sources, slots, classes, far_shift, block):
    targets, list_width = slots.shape
    operator_count = far_shift.shape[0]

    def one_block(pieces):
        slot_block, class_block = pieces
        present = slot_block >= 0
        columns = sources[:, jnp.maximum(slot_block, 0)]
        selector = (
            (class_block[..., None] == jnp.arange(operator_count, dtype=jnp.int32))
            & present[..., None]
        ).astype(jnp.float32)
        grouped = jnp.einsum("ctk,tko->otc", columns, selector, precision=highest)
        return jnp.einsum("oac,otc->at", far_shift, grouped, precision=highest)

    if targets <= block:
        return one_block((slots, classes))
    results = lax.map(
        one_block, (slots.reshape(-1, block, list_width), classes.reshape(-1, block, list_width))
    )
    return jnp.moveaxis(results, 0, 1).reshape(sources.shape[0], targets)


def near_sum(sources, targets, source_index, present, near_leaves, near_offsets, target_ids):
    leaf_count, leaf_size = (targets.shape[1], targets.shape[2])
    diagonal = jnp.eye(leaf_size, dtype=bool)

    def add_slot(entry_slot, running):
        source_rows = lax.dynamic_index_in_dim(source_index, entry_slot, 1, keepdims=False)
        neighbour = lax.dynamic_index_in_dim(near_leaves, entry_slot, 1, keepdims=False)
        counted_slot = lax.dynamic_index_in_dim(present, entry_slot, 1, keepdims=False)
        offset_class = lax.dynamic_index_in_dim(near_offsets, entry_slot, 1, keepdims=False)
        gathered = sources[:, source_rows]
        shift_x = (offset_class // 9 - 1).astype(jnp.float32)
        shift_y = (offset_class // 3 % 3 - 1).astype(jnp.float32)
        shift_z = (offset_class % 3 - 1).astype(jnp.float32)
        step_x = gathered[0][:, None, :] + shift_x[:, None, None] - targets[0][:, :, None]
        step_y = gathered[1][:, None, :] + shift_y[:, None, None] - targets[1][:, :, None]
        step_z = gathered[2][:, None, :] + shift_z[:, None, None] - targets[2][:, :, None]
        squared = step_x * step_x + step_y * step_y + step_z * step_z + softening * softening
        itself = (neighbour == target_ids) & (offset_class == 13)
        counted = counted_slot[:, None, None] & jnp.logical_not(
            itself[:, None, None] & diagonal[None]
        )
        contributions = jnp.where(counted, gathered[3][:, None, :] * lax.rsqrt(squared), 0.0)
        return running + jnp.sum(contributions, axis=2)

    return lax.fori_loop(
        0, near_leaves.shape[1], add_slot, jnp.zeros((leaf_count, leaf_size), jnp.float32)
    )


def deliver(outgoing):
    return lax.all_to_all(outgoing, ("gx", "gy"), split_axis=1, concat_axis=1, tiled=True)


def per_device(
    positions,
    charges,
    near_leaves,
    near_offsets,
    far_leaves,
    far_leaf_class,
    leaf_plan,
    far_parents,
    far_parent_class,
    parent_plan,
    coarse_lists,
    coarse_class,
    up_shift,
    down_shift,
    far_shift,
):
    coef_count = up_shift.shape[1]
    leaf_count = near_leaves.shape[0]
    leaf_size = positions.shape[1] // leaf_count
    device = lax.axis_index(("gx", "gy"))
    leaf_basis = basis(positions)
    leaf_multipoles = (leaf_basis * charges).reshape(coef_count, leaf_count, leaf_size).sum(axis=2)
    parent_multipoles = upward(leaf_multipoles, up_shift)
    grand_multipoles = upward(parent_multipoles, up_shift)
    grand_count = grand_multipoles.shape[1]
    grand_ids = device * grand_count + jnp.arange(grand_count, dtype=jnp.int32)
    coarse_count = coarse_lists.shape[0]
    lifted = jnp.einsum("gab,bg->ag", up_shift[grand_ids % 8], grand_multipoles, precision=highest)
    member = (grand_ids[:, None] // 8 == jnp.arange(coarse_count, dtype=jnp.int32)[None, :]).astype(
        jnp.float32
    )
    coarse_multipoles = lax.psum(jnp.dot(lifted, member, precision=highest), ("gx", "gy"))
    coarse_locals = far_field(coarse_multipoles, coarse_lists, coarse_class, far_shift, 256)
    grand_locals = jnp.einsum(
        "gab,bg->ag", down_shift[grand_ids % 8], coarse_locals[:, grand_ids // 8], precision=highest
    )
    leaf_capacity = leaf_plan.shape[2]
    requests = lax.all_to_all(
        jnp.concatenate([leaf_plan, parent_plan], 2),
        ("gx", "gy"),
        split_axis=1,
        concat_axis=0,
        tiled=True,
    )
    asked = jnp.maximum(requests[:, 0, :], 0)
    outgoing = jnp.concatenate(
        [
            leaf_multipoles[:, asked[:, :leaf_capacity]],
            parent_multipoles[:, asked[:, leaf_capacity:]],
        ],
        2,
    )
    arrived = deliver(outgoing)
    leaf_sources = jnp.concatenate(
        [leaf_multipoles, arrived[:, :, :leaf_capacity].reshape(coef_count, -1)], 1
    )
    parent_sources = jnp.concatenate(
        [parent_multipoles, arrived[:, :, leaf_capacity:].reshape(coef_count, -1)], 1
    )
    parent_locals = downward(grand_locals, down_shift) + far_field(
        parent_sources, far_parents, far_parent_class, far_shift, 64
    )
    leaf_locals = downward(parent_locals, down_shift) + far_field(
        leaf_sources, far_leaves, far_leaf_class, far_shift, 64
    )
    far_values = jnp.einsum(
        "alp,al->lp",
        leaf_basis.reshape(coef_count, leaf_count, leaf_size),
        leaf_locals,
        precision=highest,
    )
    particle_data = jnp.concatenate([positions, charges[None]], 0).reshape(4, leaf_count, leaf_size)
    extended = extended_2(particle_data, ((("gx", "gy"), 1),), RIM)
    first_leaf = device * leaf_count
    present = near_leaves >= 0
    source_index = jnp.where(present, near_leaves - first_leaf + RIM, 0)
    target_ids = first_leaf + jnp.arange(leaf_count, dtype=jnp.int32)
    near_values = near_sum(
        extended, particle_data, source_index, present, near_leaves, near_offsets, target_ids
    )
    return (near_values + far_values).reshape(-1)


def solution(mesh):
    placed = (
        P(None, ("gx", "gy")),
        P(("gx", "gy")),
        P(("gx", "gy"), None),
        P(("gx", "gy"), None),
        P(("gx", "gy"), None),
        P(("gx", "gy"), None),
        P(("gx", "gy"), None, None),
        P(("gx", "gy"), None),
        P(("gx", "gy"), None),
        P(("gx", "gy"), None, None),
        P(),
        P(),
        P(),
        P(),
        P(),
    )
    return jax.shard_map(
        per_device, mesh=mesh, in_specs=placed, out_specs=P(("gx", "gy")), check_vma=False
    )
```

profile of v0, /device:TPU:0, one launch (start us, length us, event | category | flops | bytes accessed | tf_op | source)
XLA Modules:
  0.0 1248.6 jit_solution(5486782208694352721)
XLA Ops:
  41.0 48.6 %gather_fusion.2 = f32[286,16384]{1,0:T(8,128)} fusion(f32[11,3,16384]{2,1,0:T(4,128)} %bitcast_dynamic-update-slice_fusion, s32[286]{0:T(512)S(1)} %copy-done.7), kind=kCustom, calls=%fused_computation.2 | custom fusion | bytes 37488880 | tf_op jit(solution)/shard_map/gather | solution.py:45
  89.6 50.1 %gather_fusion.3 = f32[286,16384]{1,0:T(8,128)} fusion(f32[11,3,16384]{2,1,0:T(4,128)} %bitcast_dynamic-update-slice_fusion, s32[286]{0:T(512)S(1)} %copy-done.6), kind=kCustom, calls=%fused_computation.3 | custom fusion | bytes 37488880 | tf_op jit(solution)/shard_map/gather | solution.py:46
  139.7 48.4 %gather_fusion.4 = f32[286,16384]{1,0:T(8,128)} fusion(f32[11,3,16384]{2,1,0:T(4,128)} %bitcast_dynamic-update-slice_fusion, s32[286]{0:T(512)S(1)} %copy-done.5), kind=kCustom, calls=%fused_computation.4 | custom fusion | bytes 37488880 | tf_op jit(solution)/shard_map/gather | solution.py:47
  188.1 18.1 %multiply_multiply_fusion = f32[286,16384]{1,0:T(8,128)S(1)} fusion(f32[286,16384]{1,0:T(8,128)} %gather_fusion.4, f32[286,16384]{1,0:T(8,128)} %gather_fusion.2, f32[286,16384]{1,0:T(8,128)} %gather_fusion.3), kind=kLoop, calls=%fused_computation.60 | loop fusion | flops 9371648 | bytes 74973184 | tf_op jit(solution)/shard_map/mul | solution.py:45
  213.7 17.5 %multiply_reduce_fusion = (f32[286,128]{1,0:T(8,128)}, f32[286,128,128]{2,1,0:T(8,128)}) fusion(f32[128,128]{1,0:T(8,128)S(1)} %bitcast.246, f32[288,128,128]{2,1,0:T(8,128)} %bitcast.226), kind=kLoop, calls=%fused_computation.61 | loop fusion | flops 9335040 | bytes 37698560 | tf_op jit(solution)/shard_map/reduce_sum | solution.py:139
  250.3 43.5 %psum.7 = f32[286,8]{0,1:T(8,128)S(1)} all-reduce(f32[286,8]{0,1:T(8,128)} %fusion.88), channel_id=1, replica_groups=mesh['gx'=4,'gy'=8] {'gx','gy'}, use_global_device_ids=true, to_apply=%region_4.5 | all-reduce | flops 2288 | bytes 18304 | tf_op jit(solution)/shard_map/psum | solution.py:149
  356.8 580.0 %while.28 = (s32[]{:T(128)}, f32[128,128]{1,0:T(8,128)}, pred[128,27]{0,1:T(8,128)(4,1)}, s32[128,27]{0,1:T(8,128)}, s32[128,27]{0,1:T(8,128)}, /*index=5*/s32[1...) while((s32[]{:T(128)}, f32[128,128]{1,0:T(8,128)}, ...), condition=%wide.region_2.3_spmd.clone, body=%wide.region_0.2_spmd.clone.sunk | while | flops 31544960 | bytes 2600203 | solution.py:108
  364.8 11.9 select_reduce_fusion.2
  386.3 11.9 select_reduce_fusion.2
  407.7 11.9 select_reduce_fusion.2
  429.2 11.9 select_reduce_fusion.2
  450.6 11.9 select_reduce_fusion.2
  472.1 11.9 select_reduce_fusion.2
  493.6 11.9 select_reduce_fusion.2
  515.0 11.9 select_reduce_fusion.2
  536.5 11.9 select_reduce_fusion.2
  558.0 11.9 select_reduce_fusion.2
  579.5 11.9 select_reduce_fusion.2
  815.8 11.9 select_reduce_fusion.2
  880.3 11.9 select_reduce_fusion.2
  901.8 11.9 select_reduce_fusion.2
  941.8 13.9 %gather_fusion.11 = f32[3024,286]{1,0:T(8,128)} fusion(f32[286,144]{0,1:T(8,128)} %pad_maximum_fusion.4, s32[3072]{0:T(1024)S(1)} %copy-done.17), kind=kCustom, calls=%fused_computation.11 | custom fusion | bytes 6931008 | tf_op jit(solution)/shard_map/gather | solution.py:68
  992.6 225.5 %while.27 = (s32[]{:T(128)}, f32[2,286,64]{1,2,0:T(8,128)}, s32[2,64,189]{2,1,0:T(8,128)}, s32[2,64,189]{2,1,0:T(8,128)}, f32[286,640]{0,1:T(8,128)S(1)}, /*index=5*/f32[16,286,286]{2,1,0:T(8,128)}, s32[]{:T(128)}) while((s32[]{:T(128)}, f32[2,286,64]{1,2,0:T(8,128)}, s32[2,64,189]{2,1,0:T(8,128)}, s32[2,64,189]{2,1,0:T(8,128)}, ...), condition=%wide.region_6.7_spmd, body=%wide.region_5.6_spmd.sunk | while | flops 1669748352 | bytes 107445320 | solution.py:78
  994.1 30.8 %gather_fusion = f32[12096,286]{1,0:T(8,128)} fusion(f32[286,640]{0,1:T(8,128)S(1)} %get-tuple-element.655, s32[12288]{0:T(1024)S(1)} %pad_clamp_fusion.10), kind=kCustom, calls=%fused_computation.1.clone.1 | custom fusion | bytes 27724032 | tf_op jit(solution)/shard_map/while/body/eval_jaxpr/gather | solution.py:68
  1024.9 17.0 %copy.225 = f32[12096,286]{0,1:T(8,128)} copy(f32[12096,286]{1,0:T(8,128)} %gather_fusion) | data formatting | bytes 27675648 | tf_op jit(solution)/shard_map/while/body/eval_jaxpr/gather | solution.py:68
  1041.9 28.2 %reshape.545 = f32[64,189,286]{1,0,2:T(8,128)} reshape(f32[12096,286]{0,1:T(8,128)} %copy.225) | data formatting | bytes 27675648 | tf_op jit(solution)/shard_map/while/body/eval_jaxpr/gather | solution.py:68
  1070.2 25.2 %fusion.116 = f32[16,64,286]{2,0,1:T(8,128)S(1)} fusion(f32[286,64,189]{2,1,0:T(8,128)} %bitcast.224, s32[64,189]{1,0:T(8,128)S(1)} %dynamic-slice_bitcast_fusion.4, pred[64,189]{1,0:T(8,128)(4,1)S(1)} %compare_bitcast_fusion.2), kind=kOutput, calls=%fused_computation.18.clone.1 | convolution fusion | flops 664602624 | bytes 15069760 | tf_op jit(solution)/shard_map/while/body/eval_jaxpr/ctk,tko->otc/dot_general | solution.py:73
  1106.6 30.8 %gather_fusion = f32[12096,286]{1,0:T(8,128)} fusion(f32[286,640]{0,1:T(8,128)S(1)} %get-tuple-element.655, s32[12288]{0:T(1024)S(1)} %pad_clamp_fusion.10), kind=kCustom, calls=%fused_computation.1.clone.1 | custom fusion | bytes 27724032 | tf_op jit(solution)/shard_map/while/body/eval_jaxpr/gather | solution.py:68
  1137.4 17.0 %copy.225 = f32[12096,286]{0,1:T(8,128)} copy(f32[12096,286]{1,0:T(8,128)} %gather_fusion) | data formatting | bytes 27675648 | tf_op jit(solution)/shard_map/while/body/eval_jaxpr/gather | solution.py:68
  1154.4 28.2 %reshape.545 = f32[64,189,286]{1,0,2:T(8,128)} reshape(f32[12096,286]{0,1:T(8,128)} %copy.225) | data formatting | bytes 27675648 | tf_op jit(solution)/shard_map/while/body/eval_jaxpr/gather | solution.py:68
  1182.7 25.2 %fusion.116 = f32[16,64,286]{2,0,1:T(8,128)S(1)} fusion(f32[286,64,189]{2,1,0:T(8,128)} %bitcast.224, s32[64,189]{1,0:T(8,128)S(1)} %dynamic-slice_bitcast_fusion.4, pred[64,189]{1,0:T(8,128)(4,1)S(1)} %compare_bitcast_fusion.2), kind=kOutput, calls=%fused_computation.18.clone.1 | convolution fusion | flops 664602624 | bytes 15069760 | tf_op jit(solution)/shard_map/while/body/eval_jaxpr/ctk,tko->otc/dot_general | solution.py:73
  1219.2 28.5 %fusion.29 = f32[128,1,128]{2,1,0:T(1,128)S(1)} fusion(f32[286,128,128]{2,1,0:T(8,128)} %get-tuple-element.481, f32[286,128,1]{0,1,2:T(8,128)S(1)} %bitcast.242), kind=kOutput, calls=%fused_computation.58 | convolution fusion | flops 56229888 | bytes 18955264 | tf_op jit(solution)/shard_map/alp,al->lp/dot_general | solution.py:183
  (487 shorter events, 608.3 us)
Async XLA Ops:
  0.0 298.5 %copy-start = (f32[8,286,286]{2,0,1:T(8,128)S(1)}, f32[8,286,286]{2,0,1:T(8,128)}, u32[]{:S(2)}) copy-start(f32[8,286,286]{2,0,1:T(8,128)} %param.38) | copy-start | bytes 7852420
  0.0 41.0 %copy-start.7 = (s32[286]{0:T(512)S(1)}, s32[286]{0:T(512)}, u32[]{:S(2)}) copy-start(s32[286]{0:T(512)} %constant.310) | copy-start | bytes 3436
  1.6 335.5 %all-to-all-start = ((s32[1,32,20]{2,0,1:T(1,128)}), s32[1,32,20]{2,0,1:T(1,128)}, u32[]{:S(2)}, u32[]{:S(2)}) async-start(s32[1,32,20]{2,0,1:T(1,128)} %copy.133), calls=%async_computation | async-start | bytes 32768 | tf_op jit(solution)/shard_map/all_to_all | solution.py:155
  10.0 0.7 copy-start.9
  12.1 342.7 %collective-permute-start = (f32[4,32,128]{2,1,0:T(8,128)}, f32[4,32,128]{2,1,0:T(8,128)}, u32[]{:S(2)}, u32[]{:S(2)}) collective-permute-start(f32[4,32,128]{2,1,0:T(8,128)} %get-tuple-element.482), channel_id=1, source_target_pairs={{0,1},{1,2},{2,3},{3,4},{4,5},{5,6},{6,7},{7,8},{8,9},{9,10},{10,1... | collective-permute-start | bytes 196616 | tf_op jit(solution)/shard_map/ppermute | solution.py:22
  14.7 340.0 %collective-permute-start.1 = (f32[4,32,128]{2,1,0:T(8,128)}, f32[4,32,128]{2,1,0:T(8,128)}, u32[]{:S(2)}, u32[]{:S(2)}) collective-permute-start(f32[4,32,128]{2,1,0:T(8,128)} %get-tuple-element.483), channel_id=1, source_target_pairs={{1,0},{2,1},{3,2},{4,3},{5,4},{6,5},{7,6},{8,7},{9,8},{10,9},{11,1... | collective-permute-start | bytes 196616 | tf_op jit(solution)/shard_map/ppermute | solution.py:23
  16.8 22.5 %copy-start.4 = (f32[3,16384]{1,0:T(4,128)S(1)}, f32[3,16384]{1,0:T(4,128)}, u32[]{:S(2)}) copy-start(f32[3,16384]{1,0:T(4,128)} %param.25) | copy-start | bytes 589828
  41.0 48.6 %copy-start.6 = (s32[286]{0:T(512)S(1)}, s32[286]{0:T(512)}, u32[]{:S(2)}) copy-start(s32[286]{0:T(512)} %constant.318) | copy-start | bytes 3436
  89.6 50.1 %copy-start.5 = (s32[286]{0:T(512)S(1)}, s32[286]{0:T(512)}, u32[]{:S(2)}) copy-start(s32[286]{0:T(512)} %constant.326) | copy-start | bytes 3436
  206.3 7.4 copy-start.12
  231.2 10.6 copy-start.23
  232.9 5.6 copy-start.3
  241.8 52.0 %copy-start.19 = (s32[8,7]{1,0:T(8,128)S(1)}, s32[8,7]{1,0:T(8,128)}, u32[]{:S(2)}) copy-start(s32[8,7]{1,0:T(8,128)} %broadcast_maximum_fusion.2) | copy-start | bytes 676
  241.8 6.9 copy-start.20
  296.9 6.5 copy-start.21
  296.9 6.5 copy-start.22
  350.0 586.8 %all-to-all-start.1 = ((f32[286,32,20]{0,2,1:T(8,128)}), f32[286,32,20]{0,2,1:T(8,128)}, u32[]{:S(2)}, u32[]{:S(2)}) async-start(f32[286,32,20]{0,2,1:T(8,128)} %pad_maximum_fusion), calls=%async_computation.1 | async-start | bytes 2359296 | tf_op jit(solution)/shard_map/all_to_all | solution.py:114
  356.8 585.0 %copy-start.17 = (s32[3072]{0:T(1024)S(1)}, s32[3072]{0:T(1024)}, u32[]{:S(2)}) copy-start(s32[3072]{0:T(1024)} %pad_clamp_fusion.2) | copy-start | bytes 36868
  961.3 8.9 copy-start.18
  961.3 16.1 %copy-start.16 = (f32[286,2,8]{0,1,2:T(2,128)S(1)}, f32[286,2,8]{0,1,2:T(2,128)}, u32[]{:S(2)}) copy-start(f32[286,2,8]{0,1,2:T(2,128)} %fusion.47) | copy-start | bytes 54916
  977.4 15.1 %copy-start.2 = (f32[286,128]{0,1:T(8,128)S(1)}, f32[286,128]{0,1:T(8,128)}, u32[]{:S(2)}) copy-start(f32[286,128]{0,1:T(8,128)} %copy.124) | copy-start | bytes 439300
  992.6 225.6 %copy-start.13 = (f32[286,16,8]{0,1,2:T(8,128)S(1)}, f32[286,16,8]{0,1,2:T(8,128)}, u32[]{:S(2)}) copy-start(f32[286,16,8]{0,1,2:T(8,128)} %fusion.44) | copy-start | bytes 439300
  1041.9 28.2 %copy-start.8 = (s32[2,64,189]{2,1,0:T(8,128)S(1)}, s32[2,64,189]{2,1,0:T(8,128)}, u32[]{:S(2)}) copy-start(s32[2,64,189]{2,1,0:T(8,128)} %get-tuple-element.654) | copy-start | bytes 290308 | tf_op jit(solution)/shard_map/while
  1041.9 28.2 %copy-start.11 = (s32[2,64,189]{2,1,0:T(8,128)S(1)}, s32[2,64,189]{2,1,0:T(8,128)}, u32[]{:S(2)}) copy-start(s32[2,64,189]{2,1,0:T(8,128)} %get-tuple-element.653) | copy-start | bytes 290308 | tf_op jit(solution)/shard_map/while
  1070.2 25.2 %copy-start.14 = (f32[2,286,64]{1,2,0:T(8,128)S(1)}, f32[2,286,64]{1,2,0:T(8,128)}, u32[]{:S(2)}) copy-start(f32[2,286,64]{1,2,0:T(8,128)} %get-tuple-element.645) | copy-start | bytes 439300 | tf_op jit(solution)/shard_map/while
  1104.8 0.7 copy-start.15
  1154.4 28.2 %copy-start.8 = (s32[2,64,189]{2,1,0:T(8,128)S(1)}, s32[2,64,189]{2,1,0:T(8,128)}, u32[]{:S(2)}) copy-start(s32[2,64,189]{2,1,0:T(8,128)} %get-tuple-element.654) | copy-start | bytes 290308 | tf_op jit(solution)/shard_map/while
  1154.4 28.2 %copy-start.11 = (s32[2,64,189]{2,1,0:T(8,128)S(1)}, s32[2,64,189]{2,1,0:T(8,128)}, u32[]{:S(2)}) copy-start(s32[2,64,189]{2,1,0:T(8,128)} %get-tuple-element.653) | copy-start | bytes 290308 | tf_op jit(solution)/shard_map/while
  1182.7 25.2 %copy-start.14 = (f32[2,286,64]{1,2,0:T(8,128)S(1)}, f32[2,286,64]{1,2,0:T(8,128)}, u32[]{:S(2)}) copy-start(f32[2,286,64]{1,2,0:T(8,128)} %get-tuple-element.645) | copy-start | bytes 439300 | tf_op jit(solution)/shard_map/while
  1217.3 0.7 copy-start.15
  1219.2 28.6 %copy-start.10 = (f32[128,128]{1,0:T(8,128)S(1)}, f32[128,128]{1,0:T(8,128)}, u32[]{:S(2)}) copy-start(f32[128,128]{1,0:T(8,128)} %get-tuple-element.320) | copy-start | bytes 196612
  1219.2 29.2 %copy-start.1 = (f32[8,286,286]{2,0,1:T(8,128)S(1)}, f32[8,286,286]{2,0,1:T(8,128)}, u32[]{:S(2)}) copy-start(f32[8,286,286]{2,0,1:T(8,128)} %param.38) | copy-start | bytes 7852420
where the time goes:
time: 1270 us; the launch traced here: 1250 us
  local copies, waits for them, and re-layouts  535 us (42%)
  other arithmetic  503 us (40%)
  matrix products  149 us (12%)
  blocking collectives  43.5 us (3%)
  starting transfers between devices  16.2 us (1%)
    reduce_sum x27, other arithmetic, add_slot(): return running + jnp.sum(contributions, axis=2)  322 us
    gather x11, local copies, waits for them, and re-layouts, one_block(): columns = sources[:, jnp.maximum(slot_block, 0)]  183 us
    gather x27, local copies, waits for them, and re-layouts, add_slot(): gathered = sources[:, source_rows]  66.2 us
    dot_general x4, matrix products, one_block(): grouped = jnp.einsum('ctk,tko->otc', columns, selector, precision=highest)  58.8 us
    gather x1, local copies, waits for them, and re-layouts, basis(): stacked[exponent_table[1], 1]  50.1 us
    gather x1, local copies, waits for them, and re-layouts, basis(): stacked[exponent_table[0], 0] * stacked[exponent_table[1], 1]  48.6 us
    gather x1, local copies, waits for them, and re-layouts, basis(): stacked[exponent_table[2], 2]  48.4 us
    slice x27, local copies, waits for them, and re-layouts, add_slot(): gathered[3][:, None, :] * lax.rsqrt(squared)  44.9 us
  transfers between devices with their start and end apart: 4, of which 0 were waited for; matrix products, arithmetic and copies ran while one was open for 70% of the time, Pallas kernels for 0%

commit v1 on v0

v1 whole, which is shorter than its diff:
```python
import functools

import jax
import jax.numpy as jnp
from jax import lax
from jax.experimental import pallas as pl
from jax.experimental.pallas import tpu as pltpu
from jax.sharding import PartitionSpec as P

ORDER = 10
RIM = 32
QUAD = 4
softening = 0.05
AXES = ("gx", "gy")
VMEM_LIMIT = 56 * 1024 * 1024
f32 = jnp.float32
bf16 = jnp.bfloat16


def exponent_index(order):
    index = {}
    for degree in range(order + 1):
        for i in range(degree, -1, -1):
            for j in range(degree - i, -1, -1):
                index[(i, j, degree - i - j)] = len(index)
    return index


INDEX = exponent_index(ORDER)
NT = (((1,), (1,)), ((), ()))


def split2(x):
    high = x.astype(bf16)
    low = (x - high.astype(f32)).astype(bf16)
    return high, low


def dot_nt(x, w):
    xh, xl = split2(x)
    wh, wl = split2(w)
    out = lax.dot_general(xh, wh, NT, preferred_element_type=f32)
    out += lax.dot_general(xl, wh, NT, preferred_element_type=f32)
    return out + lax.dot_general(xh, wl, NT, preferred_element_type=f32)


def joined(held, rows, coef):
    return jnp.concatenate([held[b, rows, :] for b in range(held.shape[0])], axis=1)[:, :coef]


def spread_to(held, rows, value):
    value = jnp.pad(value, ((0, 0), (0, held.shape[0] * 128 - value.shape[1])))
    for b in range(held.shape[0]):
        held[b, rows, :] = value[:, b * 128 : (b + 1) * 128]


def upward_kernel(ids_ref, pos_ref, chg_ref, up_ref, leaf_ref, parent_ref, lifted_ref, mom, rows, prow):
    coef = up_ref.shape[1]
    parents = parent_ref.shape[0]
    grands = parents // 8
    mom[...] = jnp.zeros_like(mom)
    xt = pos_ref[0].T * 2.0
    yt = pos_ref[1].T * 2.0
    zt = pos_ref[2].T * 2.0
    qt = chg_ref[...].T
    size = xt.shape[0]
    chunk = 64
    for start in range(0, size, chunk):
        x, y, z, wi = (v[start : start + chunk] for v in (xt, yt, zt, qt))
        for i in range(ORDER + 1):
            if i:
                wi = wi * x
            wj = wi
            for j in range(ORDER + 1 - i):
                if j:
                    wj = wj * y
                wk = wj
                for k in range(ORDER + 1 - i - j):
                    if k:
                        wk = wk * z
                    a = INDEX[(i, j, k)]
                    mom[a : a + 1, :] += jnp.sum(wk, axis=0, keepdims=True)
    for b in range(mom.shape[0] // 128):
        rows[b] = mom[b * 128 : (b + 1) * 128, :].T
    leaf_ref[...] = joined(rows, slice(None), coef)
    total = jnp.zeros((parents, coef), f32)
    for c in range(8):
        total += dot_nt(joined(rows, pl.ds(c, parents, stride=8), coef), up_ref[c])
    parent_ref[...] = total
    spread_to(prow, slice(None), total)
    grand = jnp.zeros((grands, coef), f32)
    for c in range(8):
        grand += dot_nt(joined(prow, pl.ds(c, grands, stride=8), coef), up_ref[c])
    for g in range(grands):
        lifted_ref[g : g + 1, :] = dot_nt(grand[g : g + 1], up_ref[ids_ref[g]])


def upward_call(ids, pos, chg, up):
    leaves = pos.shape[1]
    coef = up.shape[1]
    parents = leaves // 8
    wide = pl.cdiv(coef, 128) * 128
    vmem = pl.BlockSpec(memory_space=pltpu.VMEM)
    return pl.pallas_call(
        upward_kernel,
        out_shape=(
            jax.ShapeDtypeStruct((leaves, coef), f32),
            jax.ShapeDtypeStruct((parents, coef), f32),
            jax.ShapeDtypeStruct((parents // 8, coef), f32),
        ),
        in_specs=[pl.BlockSpec(memory_space=pltpu.SMEM), vmem, vmem, vmem],
        out_specs=(vmem, vmem, vmem),
        scratch_shapes=[
            pltpu.VMEM((wide, leaves), f32),
            pltpu.VMEM((wide // 128, leaves, 128), f32),
            pltpu.VMEM((wide // 128, parents, 128), f32),
        ],
        compiler_params=pltpu.CompilerParams(vmem_limit_bytes=VMEM_LIMIT),
        name="upward",
    )(ids, pos, chg, up)


def near_kernel(
    leaves, width, count_ref, src_ref, off_ref, total_ref, data_ref, table_ref, out_ref,
    targets, acc, b0, b1, r0, r1,
):
    row = lax.broadcasted_iota(jnp.int32, (8, 128), 0)
    soft = softening * softening

    def pieces(s):
        p1 = s.astype(bf16).astype(f32)
        rest = s - p1
        p2 = rest.astype(bf16).astype(f32)
        return p1, p2, rest - p2

    def set_target(l, carry):
        t = data_ref[RIM + l]
        square = jnp.sum(jnp.where(row < 3, t * t, 0.0), axis=0, keepdims=True)
        t = jnp.where(row < 3, -2.0 * t, jnp.where(row == 3, 1.0, jnp.where(row == 4, square, 0.0)))
        t1, t2, t3 = pieces(t)
        zero = jnp.zeros((80, 128), f32)
        full = jnp.concatenate([t1, t2, t3, t1, t2, t1, zero], axis=0)
        targets[l] = full.T[:, :48].astype(bf16)
        acc[l] = jnp.zeros((128, 128), f32)
        return carry

    lax.fori_loop(0, leaves, set_target, 0, unroll=4)

    def build(l, k, b):
        named = []
        for j in range(QUAD):
            entry = l * width + k + j
            m = src_ref[entry]
            s = data_ref[m] + table_ref[off_ref[entry]]
            square = jnp.sum(jnp.where(row < 3, s * s, 0.0), axis=0, keepdims=True) + soft
            s = jnp.where(row == 3, square, s)
            s1, s2, s3 = pieces(s)
            b[:, j * 128 : (j + 1) * 128] = jnp.concatenate([s1, s1, s1, s2, s2, s3], axis=0).astype(bf16)
            named.append(m)
        return tuple(named)

    def multiply(l, b, r):
        r[...] = jnp.dot(targets[jnp.minimum(l, leaves - 1)], b[...], preferred_element_type=f32)

    def collect(l, named, r):
        charges = [data_ref[m, 5:6, :] for m in named]
        for start in range(0, 128, 32):
            part = acc[l, start : start + 32, :]
            for j in range(QUAD):
                part += lax.rsqrt(r[start : start + 32, j * 128 : (j + 1) * 128]) * charges[j]
            acc[l, start : start + 32, :] = part

    def step(state, b_new, b_old, r_new, r_old):
        l, k, l1, named1, l2, named2 = state
        collect(l2, named2, r_old)
        multiply(l1, b_old, r_new)
        named = build(l, k, b_new)
        more = k + QUAD < count_ref[l]
        k_next = jnp.where(more, k + QUAD, 0)
        l_next = jnp.where(more, l, jnp.minimum(l + 1, leaves))
        return l_next, k_next, l, named, l1, named1

    def both(it, state):
        state = step(state, b0, b1, r1, r0)
        return step(state, b1, b0, r0, r1)

    none = jnp.int32(leaves)
    empty = (jnp.int32(data_ref.shape[0] - 1),) * QUAD
    start = (jnp.int32(0), jnp.int32(0), none, empty, none, empty)
    lax.fori_loop(0, (total_ref[0] + 3) // 2, both, start)

    lane = lax.broadcasted_iota(jnp.int32, (128, 128), 1)
    out_ref[...] = jnp.zeros_like(out_ref)

    def finish(l, carry):
        total = jnp.sum(acc[l], axis=1, keepdims=True)
        out_ref[...] = jnp.where(lane == l, total, out_ref[...])
        return carry

    lax.fori_loop(0, leaves, finish, 0, unroll=8)


def near_call(counts, sources, offsets, total, data, table, leaves, width):
    vmem = pl.BlockSpec(memory_space=pltpu.VMEM)
    smem = pl.BlockSpec(memory_space=pltpu.SMEM)
    pairs = leaves * 18 * 128 * 128
    return pl.pallas_call(
        functools.partial(near_kernel, leaves, width),
        out_shape=jax.ShapeDtypeStruct((128, leaves), f32),
        in_specs=[smem, smem, smem, smem, vmem, vmem],
        out_specs=vmem,
        scratch_shapes=[
            pltpu.VMEM((leaves, 128, 48), bf16),
            pltpu.VMEM((leaves + 1, 128, 128), f32),
            pltpu.VMEM((48, QUAD * 128), bf16),
            pltpu.VMEM((48, QUAD * 128), bf16),
            pltpu.VMEM((128, QUAD * 128), f32),
            pltpu.VMEM((128, QUAD * 128), f32),
        ],
        compiler_params=pltpu.CompilerParams(vmem_limit_bytes=VMEM_LIMIT),
        cost_estimate=pl.CostEstimate(flops=pairs * 96, bytes_accessed=1 << 20, transcendentals=pairs),
        name="near",
    )(counts, sources, offsets, total, data, table)


def count_kernel(blocks, slot_ref, class_ref, out_ref, high, low, held):
    targets, width = slot_ref.shape
    heights = held.shape[0] // targets
    slots = slot_ref[...]
    high[...] = jnp.where(slots >= 0, class_ref[...] * blocks + slots // 128, -1)
    low[...] = jnp.where(slots >= 0, slots % 128, -1)
    high_row = lax.broadcasted_iota(jnp.int32, (heights, width), 0)
    low_row = lax.broadcasted_iota(jnp.int32, (128, width), 0)

    def one(t, carry):
        h = (high_row == high[pl.ds(t, 1), :]).astype(f32).astype(bf16)
        w = (low_row == low[pl.ds(t, 1), :]).astype(f32).astype(bf16)
        held[pl.ds(t, heights, stride=targets), :] = lax.dot_general(h, w, NT, preferred_element_type=f32)
        return carry

    lax.fori_loop(0, targets, one, 0, unroll=4)
    out_ref[...] = held[...].astype(bf16)


def count_call(slots, classes, blocks, operators):
    targets, width = slots.shape
    vmem = pl.BlockSpec(memory_space=pltpu.VMEM)
    rows = operators * blocks * targets
    held = pl.pallas_call(
        functools.partial(count_kernel, blocks),
        out_shape=jax.ShapeDtypeStruct((rows, 128), bf16),
        in_specs=[vmem, vmem],
        out_specs=vmem,
        scratch_shapes=[
            pltpu.VMEM((targets, width), jnp.int32),
            pltpu.VMEM((targets, width), jnp.int32),
            pltpu.VMEM((rows, 128), f32),
        ],
        compiler_params=pltpu.CompilerParams(vmem_limit_bytes=VMEM_LIMIT),
        cost_estimate=pl.CostEstimate(
            flops=targets * 2 * 256 * 128 * operators * blocks, bytes_accessed=rows * 256, transcendentals=0
        ),
        name="count",
    )(slots, classes)
    return held.reshape(operators, blocks, targets, 128)


def far_kernel(
    grands, ids_ref, lc_ref, pc_ref, cc_ref, own_ref, got_ref, pown_ref, pgot_ref, coarse_ref,
    shift_ref, down_ref, pos_ref, chg_ref, self_ref, near_ref, out_ref,
    leaf_src, parent_src, coarse_src, total, wide, spread, held,
):
    o = pl.program_id(0)
    leaves, coef = own_ref.shape
    parents = pown_ref.shape[0]
    coarse = coarse_ref.shape[0]

    @pl.when(o == 0)
    def _():
        total[...] = jnp.zeros_like(total)
        leaf_src[...] = jnp.zeros_like(leaf_src)
        parent_src[...] = jnp.zeros_like(parent_src)
        for target, first, second in ((leaf_src, own_ref, got_ref), (parent_src, pown_ref, pgot_ref)):
            n = first.shape[0]
            for side, half in enumerate(split2(first[...])):
                target[side, :n, :] = half
            for side, half in enumerate(split2(second[...])):
                target[side, n : n + second.shape[0], :] = half
        for side, half in enumerate(split2(coarse_ref[...])):
            coarse_src[side] = half

    def grouped(counts, source):
        lhs = jnp.concatenate([counts[0, b] for b in range(counts.shape[1])], axis=1)
        return jnp.dot(lhs, source[0], preferred_element_type=f32) + jnp.dot(
            lhs, source[1], preferred_element_type=f32
        )

    few = cc_ref[0].astype(bf16)
    small = jnp.dot(few, coarse_src[0], preferred_element_type=f32) + jnp.dot(
        few, coarse_src[1], preferred_element_type=f32
    )
    stacked = jnp.concatenate([grouped(lc_ref, leaf_src), grouped(pc_ref, parent_src), small], axis=0)
    total[...] += dot_nt(stacked, shift_ref[0])

    @pl.when(o == pl.num_programs(0) - 1)
    def _():
        far_parent = total[leaves : leaves + parents, :]
        far_coarse = total[leaves + parents :, :]
        rows = lax.broadcasted_iota(jnp.int32, (coarse, coef), 0)
        grand_rows = []
        for g in range(grands):
            mine = jnp.sum(jnp.where(rows == ids_ref[grands + g], far_coarse, 0.0), axis=0, keepdims=True)
            grand_rows.append(dot_nt(mine, down_ref[ids_ref[g]]))
        grand = jnp.concatenate(grand_rows, axis=0)
        for c in range(8):
            spread_to(spread, pl.ds(c, grands, stride=8), dot_nt(grand, down_ref[c]))
        parent = joined(spread, slice(None), coef) + far_parent
        for c in range(8):
            spread_to(wide, pl.ds(c, parents, stride=8), dot_nt(parent, down_ref[c]))
        loc = joined(wide, slice(None), coef) + total[:leaves, :]
        spread_to(wide, slice(None), loc)
        for b in range(wide.shape[0]):
            held[b * 128 : (b + 1) * 128, :] = wide[b].T
        xt = pos_ref[0].T * 2.0
        yt = pos_ref[1].T * 2.0
        zt = pos_ref[2].T * 2.0
        chunk = 64
        outs = []
        for start in range(0, xt.shape[0], chunk):
            x, y, z = (v[start : start + chunk] for v in (xt, yt, zt))
            pot = None
            for i in range(ORDER, -1, -1):
                mid = None
                for j in range(ORDER - i, -1, -1):
                    low = None
                    for k in range(ORDER - i - j, -1, -1):
                        a = INDEX[(i, j, k)]
                        value = held[a : a + 1, :]
                        low = jnp.broadcast_to(value, x.shape) if low is None else low * z + value
                    mid = low if mid is None else mid * y + low
                pot = mid if pot is None else pot * x + mid
            outs.append(pot)
        far = jnp.concatenate(outs, axis=0)
        alone = self_ref[...] * (1.0 / softening)
        out_ref[...] = (far + near_ref[...] - chg_ref[...].T * alone).T


def far_call(ids, lc, pc, cc, own, got, pown, pgot, coarse, shift, down, pos, chg, alone, near):
    operators, coef = shift.shape[:2]
    leaves, parents, ncoarse = own.shape[0], pown.shape[0], coarse.shape[0]
    vmem = pl.BlockSpec(memory_space=pltpu.VMEM)
    smem = pl.BlockSpec(memory_space=pltpu.SMEM)
    wide = pl.cdiv(coef, 128) * 128

    def per_operator(x):
        return pl.BlockSpec((1,) + x.shape[1:], lambda o: (o,) + (0,) * (x.ndim - 1))

    return pl.pallas_call(
        functools.partial(far_kernel, parents // 8),
        grid=(operators,),
        out_shape=jax.ShapeDtypeStruct((leaves, 128), f32),
        in_specs=[
            smem, per_operator(lc), per_operator(pc), per_operator(cc), vmem, vmem, vmem, vmem, vmem,
            per_operator(shift), vmem, vmem, vmem, vmem, vmem,
        ],
        out_specs=vmem,
        scratch_shapes=[
            pltpu.VMEM((2, lc.shape[1] * 128, coef), bf16),
            pltpu.VMEM((2, pc.shape[1] * 128, coef), bf16),
            pltpu.VMEM((2, ncoarse, coef), bf16),
            pltpu.VMEM((leaves + parents + ncoarse, coef), f32),
            pltpu.VMEM((wide // 128, leaves, 128), f32),
            pltpu.VMEM((wide // 128, parents, 128), f32),
            pltpu.VMEM((wide, leaves), f32),
        ],
        compiler_params=pltpu.CompilerParams(vmem_limit_bytes=VMEM_LIMIT),
        name="far",
    )(ids, lc, pc, cc, own, got, pown, pgot, coarse, shift, down, pos, chg, alone, near)


def per_device(
    positions, charges, near_leaves, near_offsets, far_leaves, far_leaf_class, leaf_plan,
    far_parents, far_parent_class, parent_plan, coarse_lists, coarse_class, up_shift, down_shift, far_shift,
):
    coef = up_shift.shape[1]
    operators = far_shift.shape[0]
    leaves, width = near_leaves.shape
    parents = far_parents.shape[0]
    size = positions.shape[1] // leaves
    ncoarse = coarse_lists.shape[0]
    device = lax.axis_index(AXES)
    devices = lax.axis_size(AXES)
    grands = parents // 8
    grand_ids = device * grands + jnp.arange(grands, dtype=jnp.int32)
    ids = jnp.concatenate([grand_ids % 8, grand_ids // 8])

    pos = positions.reshape(3, leaves, size)
    chg = charges.reshape(leaves, size)

    cap_l, cap_p = leaf_plan.shape[2], parent_plan.shape[2]
    requests = lax.all_to_all(
        jnp.concatenate([leaf_plan, parent_plan], 2), AXES, split_axis=1, concat_axis=0, tiled=True
    )
    asked = jnp.maximum(requests[:, 0, :], 0)

    zero = jnp.zeros((leaves, 1, size), f32)
    data = jnp.concatenate(
        [jnp.moveaxis(pos, 0, 1), zero, zero + 1.0, chg[:, None, :], zero, zero], axis=1
    )
    up = [(i, i + 1) for i in range(devices - 1)]
    down = [(j, i) for i, j in up]
    before = lax.ppermute(data[leaves - RIM :], AXES, up)
    after = lax.ppermute(data[:RIM], AXES, down)

    leaf_rows, parent_rows, lifted = upward_call(ids, pos, chg, up_shift)

    outgoing = jnp.concatenate([leaf_rows[asked[:, :cap_l]], parent_rows[asked[:, cap_l:]]], axis=1)
    arrived = lax.all_to_all(outgoing, AXES, split_axis=0, concat_axis=0, tiled=True)
    member = (
        jnp.arange(ncoarse, dtype=jnp.int32)[:, None] == grand_ids[None, :] // 8
    ).astype(f32)
    coarse = lax.psum(jnp.sum(member[:, :, None] * lifted[None], axis=1), AXES)

    extended = jnp.concatenate([before, data, after, jnp.zeros((1, 8, size), f32)], axis=0)
    present = near_leaves >= 0
    first = device * leaves
    padded = pl.cdiv(width, QUAD) * QUAD
    source = jnp.where(present, near_leaves - first + RIM, leaves + 2 * RIM)
    source = jnp.pad(source, ((0, 1), (0, padded - width)), constant_values=leaves + 2 * RIM).reshape(-1)
    offset = jnp.pad(jnp.where(present, near_offsets, 13), ((0, 1), (0, padded - width)), constant_values=13).reshape(-1)
    counts = jnp.pad(jnp.sum(present.astype(jnp.int32), axis=1), (0, 1))
    total = jnp.sum((counts + QUAD - 1) // QUAD, keepdims=True)
    classes = jnp.arange(27, dtype=jnp.int32)
    shifts = jnp.stack([classes // 9 - 1, classes // 3 % 3 - 1, classes % 3 - 1], axis=1).astype(f32)
    table = jnp.broadcast_to(jnp.pad(shifts, ((0, 0), (0, 5)))[:, :, None], (27, 8, size))
    near = near_call(counts, source, offset, total, extended, table, leaves, padded)
    target_ids = first + jnp.arange(leaves, dtype=jnp.int32)
    alone = jnp.sum(
        ((near_leaves == target_ids[:, None]) & (near_offsets == 13)).astype(f32), axis=1
    )[None, :]

    leaf_blocks = pl.cdiv(leaves + devices * cap_l, 128)
    parent_blocks = pl.cdiv(parents + devices * cap_p, 128)
    lc = count_call(far_leaves, far_leaf_class, leaf_blocks, operators)
    pc = count_call(far_parents, far_parent_class, parent_blocks, operators)
    hit = coarse_class[None] == jnp.arange(operators, dtype=jnp.int32)[:, None, None]
    where = coarse_lists[:, :, None] == jnp.arange(ncoarse, dtype=jnp.int32)
    cc = jnp.sum((hit[..., None] & where[None]).astype(f32), axis=2)
    out = far_call(
        ids, lc, pc, cc, leaf_rows, arrived[:, :cap_l].reshape(-1, coef), parent_rows,
        arrived[:, cap_l:].reshape(-1, coef), coarse, far_shift, down_shift, pos, chg, alone, near,
    )
    return out.reshape(-1)


def solution(mesh):
    one, two, three = P(AXES), P(AXES, None), P(AXES, None, None)
    placed = (
        P(None, AXES), one, two, two, two, two, three, two, two, three, P(), P(), P(), P(), P(),
    )
    return jax.shard_map(per_device, mesh=mesh, in_specs=placed, out_specs=one, check_vma=False)
```

time: 1270 us -> 229 us (0.18); the launches traced: 1250 us -> 226 us
  local copies, waits for them, and re-layouts: 535 us -> 31.3 us
  other arithmetic: 503 us -> 5.63 us
  matrix products: 149 us -> 0 us
  Pallas kernels: 0 us -> 130 us
    gather x47 -> x3, local copies, waits for them, and re-layouts: 414 us -> 3.23 us  [the longest x2 1.64 us: per_device(): parent_rows[asked[:, cap_l:]]]
    reduce_sum x28 -> x4, other arithmetic: 340 us -> 2.69 us  [the longest x1 1.17 us: per_device(): total = jnp.sum((counts + QUAD - 1) // QUAD, keepdims=True)]
    dot_general x16 -> x0, matrix products: 149 us -> none  [the longest x4 58.8 us: one_block(): grouped = jnp.einsum('ctk,tko->otc', columns, selector, precision=highest)]
    pallas_call x0 -> x5, Pallas kernels: none -> 130 us  [the longest x1 79.3 us: near_call(): pl.pallas_call(functools.partial(near_kernel, leaves, width), out_shape=j...]
    slice x29 -> x3, local copies, waits for them, and re-layouts: 47.8 us -> 1 us  [the longest x1 0.96 us: per_device(): arrived[:, :cap_l].reshape(-1, coef)]
    add x82 -> x1, other arithmetic: 46.5 us -> 0.01 us  [per_device(): target_ids = first + jnp.arange(leaves, dtype=jnp.int32)]
    sub x27 -> x0, local copies, waits for them, and re-layouts: 24.7 us -> none  [add_slot(): gathered[0][:, None, :] + shift_x[:, None, None] - targets[0][:, :, None]]
    select_n x33 -> x4, other arithmetic: 22.2 us -> 0.12 us  [the longest x1 0.07 us: per_device(): parent_rows[asked[:, cap_l:]]]
  transfers between devices with their start and end apart: 4 -> 4, of which waited for: 0 -> 0; matrix products, arithmetic and copies ran while one was open for 70% -> 15% of each run, Pallas kernels for 0% -> 47%
where the time goes in v1:
time: 229 us; the launch traced here: 226 us
  Pallas kernels  130 us (57%)
  blocking collectives  40.4 us (18%)
  local copies, waits for them, and re-layouts  31.3 us (14%)
  starting transfers between devices  18.9 us (8%)
  other arithmetic  5.63 us (2%)
    pallas_call x1, Pallas kernels, near_call(): pl.pallas_call(functools.partial(near_kernel, leaves, width), out_shape=j...  79.3 us
    psum x1, blocking collectives, per_device(): coarse = lax.psum(jnp.sum(member[:, :, None] * lifted[None], axis=1), AXES)  40.4 us
    pallas_call x1, Pallas kernels, far_call(): pl.pallas_call(functools.partial(far_kernel, parents // 8), grid=(operato...  24.4 us
    unnamed x26, local copies, waits for them, and re-layouts  21.5 us
    pallas_call x2, Pallas kernels, count_call(): pl.pallas_call(functools.partial(count_kernel, blocks), out_shape=jax.Sha...  14.6 us
    pallas_call x1, Pallas kernels, upward_call(): pl.pallas_call(upward_kernel, out_shape=(jax.ShapeDtypeStruct((leaves, co...  11.4 us
    all_to_all x1, starting transfers between devices, per_device(): lax.all_to_all(outgoing, AXES, split_axis=0, concat_axis=0, tiled=True)  8.12 us
    all_to_all x1, starting transfers between devices, per_device(): lax.all_to_all(jnp.concatenate([leaf_plan, parent_plan], 2), AXES, split_...  7.3 us
  transfers between devices with their start and end apart: 4, of which 0 were waited for; matrix products, arithmetic and copies ran while one was open for 15% of the time, Pallas kernels for 47%

profile of v1, /device:TPU:0, one launch (start us, length us, event | category | flops | bytes accessed | tf_op | source)
XLA Modules:
  0.0 226.1 jit_solution(59487696425421559)
XLA Ops:
  0.0 0.7 pad_add_fusion
  0.7 0.7 copy.57
  1.4 7.3 %all-to-all-start = ((s32[1,32,20]{2,0,1:T(1,128)}), s32[1,32,20]{2,0,1:T(1,128)S(1)}, u32[]{:S(2)}, u32[]{:S(2)}) async-start(s32[1,32,20]{2,0,1:T(1,128)} %copy.57), calls=%async_computation | async-start | bytes 32768 | tf_op jit(solution)/shard_map/all_to_all | solution.py:401
  8.7 1.7 bitcast_dynamic-update-slice_fusion
  10.4 0.8 bitcast_dynamic-update-slice_fusion.1
  11.3 2.2 collective-permute-start
  13.5 1.3 collective-permute-start.1
  15.5 4.4 %copy.56.up_ref = f32[8,286,286]{2,1,0:T(8,128)} copy(f32[8,286,286]{2,0,1:T(8,128)} %param.27) | data formatting | bytes 5234944 | tf_op args[12]
  19.9 11.4 %upward.1 = (f32[128,286]{1,0:T(8,128)}, f32[16,286]{1,0:T(8,128)}, f32[2,286]{1,0:T(2,128)}) custom-call(s32[4]{0:T(128)} %pad_add_fusion.1.ids_ref, f32[3,128,128]{2,1,0:T(8,128)} %get-tuple-element.12.pos_ref, f32[128,128]{1,0:T(8,128)} %bitcast.21, f32[8,286,286]{2,1,0:T(8,128)} %copy.56.up_ref), custom_call_target="tpu_custom_call" | custom-call | tf_op jit(solution)/shard_map/upward/pallas_call | solution.py:104
  31.3 0.8 multiply_reduce_fusion
  32.2 1.2 fusion
  33.3 0.8 copy.54.slot_ref
  34.1 0.7 copy.55.class_ref
  35.1 1.6 gather_fusion.1
  36.8 1.6 gather_fusion
  38.4 1.1 pad_maximum_fusion
  39.5 8.1 %all-to-all-start.1 = ((f32[32,20,286]{2,1,0:T(8,128)}), f32[32,20,286]{2,1,0:T(8,128)S(1)}, u32[]{:S(2)}, u32[]{:S(2)}) async-start(f32[32,20,286]{2,1,0:T(8,128)} %pad_maximum_fusion), calls=%async_computation.1 | async-start | bytes 2359296 | tf_op jit(solution)/shard_map/all_to_all | solution.py:418
  48.0 12.4 %count.2 = bf16[10240,128]{1,0:T(8,128)(2,1)} custom-call(s32[128,189]{1,0:T(8,128)} %copy.54.slot_ref, s32[128,189]{1,0:T(8,128)} %copy.55.class_ref), custom_call_target="tpu_custom_call" | custom-call | flops 671088640 | bytes 2621440 | tf_op jit(solution)/shard_map/count/pallas_call | solution.py:249
  60.4 0.7 copy.62.cc_ref
  61.2 0.7 reshape.210.off_ref
  62.1 0.7 reshape.209.src_ref
  62.8 4.5 %copy.64.down_ref = f32[8,286,286]{2,1,0:T(8,128)} copy(f32[8,286,286]{2,0,1:T(8,128)} %param.28) | data formatting | bytes 5234944 | tf_op args[13]
  67.3 8.2 %copy.63.shift_ref = f32[16,286,286]{2,1,0:T(8,128)} copy(f32[16,286,286]{2,0,1:T(8,128)} %param.29) | data formatting | bytes 10469888 | tf_op args[14]
  75.5 40.4 %psum.7.coarse_ref = f32[8,286]{1,0:T(8,128)} all-reduce(f32[8,286]{1,0:T(8,128)S(1)} %multiply_reduce_fusion), channel_id=1, replica_groups=mesh['gx'=4,'gy'=8] {'gx','gy'}, use_global_device_ids=true, to_apply=%region_2.3 | all-reduce | flops 2288 | bytes 18304 | tf_op jit(solution)/shard_map/psum | solution.py:422
  116.0 2.2 count.3
  118.2 0.6 convert_reduce_fusion.2
  119.0 1.0 copy.61.data_ref
  120.0 0.7 broadcast_in_dim.47.table_ref
  120.7 79.3 %near.1.near_ref = f32[128,128]{1,0:T(8,128)} custom-call(s32[129]{0:T(256)} %get-tuple-element.19.count_ref, s32[3612]{0:T(1024)} %reshape.209.src_ref, s32[3612]{0:T(1024)} %reshape.210.off_ref, s32[1]{0:T(128)} %bitcast.7.total_ref, f32[193,8,128]{2,1,0:T(8,128)} %copy.61.data_ref, f32[27,8,128]{2,1,0:T(8,128)} %broadcast_in_dim.47.table_ref), custom_call_target="tpu_custom_call" | custom-call | flops 3623878656 | bytes 1048576 | tf_op jit(solution)/shard_map/near/pallas_call | solution.py:207
  200.0 0.7 reshape.208.pgot_ref
  200.8 1.0 slice.30
  201.7 24.4 %far.1 = f32[128,128]{1,0:T(8,128)} custom-call(s32[4]{0:T(128)} %pad_add_fusion.1.ids_ref, bf16[16,5,128,128]{3,2,1,0:T(8,128)(2,1)} %bitcast.18, bf16[16,2,16,128]{3,2,1,0:T(8,128)(2,1)} %bitcast.23, f32[16,8,8]{2,1,0:T(8,128)} %copy.62.cc_ref, f32[128,286]{1,0:T(8,128)} %get-tuple-element.8.own_ref, f32[512,286]{1,0:T(8,128)} %bitcast.19, ...), custom_call_target="tpu_custom_call" | custom-call | tf_op jit(solution)/shard_map/far/pallas_call | solution.py:358
  (49 shorter events, 2.0 us)
Async XLA Ops:
  1.4 33.4 %all-to-all-start = ((s32[1,32,20]{2,0,1:T(1,128)}), s32[1,32,20]{2,0,1:T(1,128)S(1)}, u32[]{:S(2)}, u32[]{:S(2)}) async-start(s32[1,32,20]{2,0,1:T(1,128)} %copy.57), calls=%async_computation | async-start | bytes 32768 | tf_op jit(solution)/shard_map/all_to_all | solution.py:401
  11.3 107.5 %collective-permute-start = (f32[32,8,128]{2,0,1:T(8,128)S(1)}, f32[32,8,128]{2,0,1:T(8,128)S(1)}, u32[]{:S(2)}, u32[]{:S(2)}) collective-permute-start(f32[32,8,128]{2,0,1:T(8,128)S(1)} %get-tuple-element.13), channel_id=1, source_target_pairs={{0,1},{1,2},{2,3},{3,4},{4,5},{5,6},{6,7},{7,8},{8,9},{9,10},{10,1... | collective-permute-start | bytes 393224 | tf_op jit(solution)/shard_map/ppermute | solution.py:412
  13.5 105.4 %collective-permute-start.1 = (f32[32,8,128]{2,0,1:T(8,128)S(1)}, f32[32,8,128]{2,0,1:T(8,128)S(1)}, u32[]{:S(2)}, u32[]{:S(2)}) collective-permute-start(f32[32,8,128]{2,0,1:T(8,128)S(1)} %get-tuple-element.14), channel_id=1, source_target_pairs={{1,0},{2,1},{3,2},{4,3},{5,4},{6,5},{7,6},{8,7},{9,8},{10,9},{11,1... | collective-permute-start | bytes 393224 | tf_op jit(solution)/shard_map/ppermute | solution.py:413
  19.9 12.2 %copy-start.3 = (s32[128,27]{0,1:T(8,128)S(1)}, s32[128,27]{0,1:T(8,128)}, u32[]{:S(2)}) copy-start(s32[128,27]{0,1:T(8,128)} %param.18) | copy-start | bytes 41476
  19.9 12.2 %copy-start.4 = (s32[128,27]{0,1:T(8,128)S(1)}, s32[128,27]{0,1:T(8,128)}, u32[]{:S(2)}) copy-start(s32[128,27]{0,1:T(8,128)} %param.17) | copy-start | bytes 41476
  19.9 13.4 %copy-start.1 = (s32[128,189]{0,1:T(8,128)S(1)}, s32[128,189]{0,1:T(8,128)}, u32[]{:S(2)}) copy-start(s32[128,189]{0,1:T(8,128)} %param.19) | copy-start | bytes 290308
  19.9 14.2 %copy-start.2 = (s32[128,189]{0,1:T(8,128)S(1)}, s32[128,189]{0,1:T(8,128)}, u32[]{:S(2)}) copy-start(s32[128,189]{0,1:T(8,128)} %param.20) | copy-start | bytes 290308
  31.3 5.5 %copy-start = (f32[128,286]{1,0:T(8,128)S(1)}, f32[128,286]{1,0:T(8,128)}, u32[]{:S(2)}) copy-start(f32[128,286]{1,0:T(8,128)} %get-tuple-element.8.own_ref) | copy-start | bytes 439300
  38.4 9.3 %copy-start.5 = (s32[8,7]{1,0:T(8,128)S(1)}, s32[8,7]{1,0:T(8,128)}, u32[]{:S(2)}) copy-start(s32[8,7]{1,0:T(8,128)} %param.25) | copy-start | bytes 676
  38.4 9.3 %copy-start.6 = (s32[8,7]{1,0:T(8,128)S(1)}, s32[8,7]{1,0:T(8,128)}, u32[]{:S(2)}) copy-start(s32[8,7]{1,0:T(8,128)} %param.26) | copy-start | bytes 676
  39.5 160.5 %all-to-all-start.1 = ((f32[32,20,286]{2,1,0:T(8,128)}), f32[32,20,286]{2,1,0:T(8,128)S(1)}, u32[]{:S(2)}, u32[]{:S(2)}) async-start(f32[32,20,286]{2,1,0:T(8,128)} %pad_maximum_fusion), calls=%async_computation.1 | async-start | bytes 2359296 | tf_op jit(solution)/shard_map/all_to_all | solution.py:418

commit v2 on v1

--- a/solution.py
+++ b/solution.py
@@ -10,6 +10,7 @@
 ORDER = 10
 RIM = 32
 QUAD = 4
+GROUP = 4
 softening = 0.05
 AXES = ("gx", "gy")
 VMEM_LIMIT = 56 * 1024 * 1024
@@ -54,10 +55,13 @@
         held[b, rows, :] = value[:, b * 128 : (b + 1) * 128]
 
 
-def upward_kernel(ids_ref, pos_ref, chg_ref, up_ref, leaf_ref, parent_ref, lifted_ref, mom, rows, prow):
-    coef = up_ref.shape[1]
+def upward_kernel(ids_ref, pos_ref, chg_ref, up_ref, leaf_ref, parent_ref, lifted_ref, mom, rows, prow, up, sems):
+    coef = up.shape[1]
     parents = parent_ref.shape[0]
     grands = parents // 8
+    copies = [pltpu.make_async_copy(up_ref.at[:, c, :], up.at[c], sems.at[c]) for c in range(8)]
+    for copy in copies:
+        copy.start()
     mom[...] = jnp.zeros_like(mom)
     xt = pos_ref[0].T * 2.0
     yt = pos_ref[1].T * 2.0
@@ -85,19 +89,20 @@
     leaf_ref[...] = joined(rows, slice(None), coef)
     total = jnp.zeros((parents, coef), f32)
     for c in range(8):
-        total += dot_nt(joined(rows, pl.ds(c, parents, stride=8), coef), up_ref[c])
+        copies[c].wait()
+        total += dot_nt(joined(rows, pl.ds(c, parents, stride=8), coef), up[c])
     parent_ref[...] = total
     spread_to(prow, slice(None), total)
     grand = jnp.zeros((grands, coef), f32)
     for c in range(8):
-        grand += dot_nt(joined(prow, pl.ds(c, grands, stride=8), coef), up_ref[c])
+        grand += dot_nt(joined(prow, pl.ds(c, grands, stride=8), coef), up[c])
     for g in range(grands):
-        lifted_ref[g : g + 1, :] = dot_nt(grand[g : g + 1], up_ref[ids_ref[g]])
+        lifted_ref[g : g + 1, :] = dot_nt(grand[g : g + 1], up[ids_ref[g]])
 
 
 def upward_call(ids, pos, chg, up):
     leaves = pos.shape[1]
-    coef = up.shape[1]
+    coef = up.shape[0]
     parents = leaves // 8
     wide = pl.cdiv(coef, 128) * 128
     vmem = pl.BlockSpec(memory_space=pltpu.VMEM)
@@ -108,12 +113,14 @@
             jax.ShapeDtypeStruct((parents, coef), f32),
             jax.ShapeDtypeStruct((parents // 8, coef), f32),
         ),
-        in_specs=[pl.BlockSpec(memory_space=pltpu.SMEM), vmem, vmem, vmem],
+        in_specs=[pl.BlockSpec(memory_space=pltpu.SMEM), vmem, vmem, pl.BlockSpec(memory_space=pl.ANY)],
         out_specs=(vmem, vmem, vmem),
         scratch_shapes=[
             pltpu.VMEM((wide, leaves), f32),
             pltpu.VMEM((wide // 128, leaves, 128), f32),
             pltpu.VMEM((wide // 128, parents, 128), f32),
+            pltpu.VMEM((8, coef, coef), f32),
+            pltpu.SemaphoreType.DMA((8,)),
         ],
         compiler_params=pltpu.CompilerParams(vmem_limit_bytes=VMEM_LIMIT),
         name="upward",
@@ -121,9 +128,16 @@
 
 
 def near_kernel(
-    leaves, width, count_ref, src_ref, off_ref, total_ref, data_ref, table_ref, out_ref,
-    targets, acc, b0, b1, r0, r1,
+    leaves, width, count_ref, src_ref, off_ref, total_ref, data_ref, table_ref, shift_ref, out_ref, order_ref,
+    targets, acc, sems, *held,
 ):
+    bs, rs = held[:GROUP], held[GROUP:]
+    copies = [
+        pltpu.make_async_copy(shift_ref.at[:, o, :], order_ref.at[o], sems.at[o])
+        for o in range(shift_ref.shape[1])
+    ]
+    for copy in copies:
+        copy.start()
     row = lax.broadcasted_iota(jnp.int32, (8, 128), 0)
     soft = softening * softening
 
@@ -170,57 +184,63 @@
                 part += lax.rsqrt(r[start : start + 32, j * 128 : (j + 1) * 128]) * charges[j]
             acc[l, start : start + 32, :] = part
 
-    def step(state, b_new, b_old, r_new, r_old):
-        l, k, l1, named1, l2, named2 = state
-        collect(l2, named2, r_old)
-        multiply(l1, b_old, r_new)
-        named = build(l, k, b_new)
-        more = k + QUAD < count_ref[l]
-        k_next = jnp.where(more, k + QUAD, 0)
-        l_next = jnp.where(more, l, jnp.minimum(l + 1, leaves))
-        return l_next, k_next, l, named, l1, named1
-
-    def both(it, state):
-        state = step(state, b0, b1, r1, r0)
-        return step(state, b1, b0, r0, r1)
-
-    none = jnp.int32(leaves)
-    empty = (jnp.int32(data_ref.shape[0] - 1),) * QUAD
-    start = (jnp.int32(0), jnp.int32(0), none, empty, none, empty)
-    lax.fori_loop(0, (total_ref[0] + 3) // 2, both, start)
+    def body(it, state):
+        l, k, old, older = state
+        for u in range(GROUP):
+            collect(older[u][0], older[u][1], rs[u])
+        for u in range(GROUP):
+            multiply(old[u][0], bs[u], rs[u])
+        new = []
+        for u in range(GROUP):
+            new.append((l, build(l, k, bs[u])))
+            more = k + QUAD < count_ref[l]
+            k = jnp.where(more, k + QUAD, 0)
+            l = jnp.where(more, l, jnp.minimum(l + 1, leaves))
+        return l, k, tuple(new), old
+
+    none = ((jnp.int32(leaves), (jnp.int32(data_ref.shape[0] - 1),) * QUAD),) * GROUP
+    start = (jnp.int32(0), jnp.int32(0), none, none)
+    lax.fori_loop(0, (total_ref[0] + GROUP - 1) // GROUP + 2, body, start)
 
     lane = lax.broadcasted_iota(jnp.int32, (128, 128), 1)
     out_ref[...] = jnp.zeros_like(out_ref)
 
-    def finish(l, carry):
-        total = jnp.sum(acc[l], axis=1, keepdims=True)
-        out_ref[...] = jnp.where(lane == l, total, out_ref[...])
+    def finish(it, carry):
+        out = out_ref[...]
+        for u in range(8):
+            l = it * 8 + u
+            out = jnp.where(lane == l, jnp.sum(acc[l], axis=1, keepdims=True), out)
+        out_ref[...] = out
         return carry
 
-    lax.fori_loop(0, leaves, finish, 0, unroll=8)
-
-
-def near_call(counts, sources, offsets, total, data, table, leaves, width):
+    lax.fori_loop(0, leaves // 8, finish, 0)
+    for copy in copies:
+        copy.wait()
+
+
+def near_call(counts, sources, offsets, total, data, table, shift, leaves, width):
     vmem = pl.BlockSpec(memory_space=pltpu.VMEM)
     smem = pl.BlockSpec(memory_space=pltpu.SMEM)
     pairs = leaves * 18 * 128 * 128
     return pl.pallas_call(
         functools.partial(near_kernel, leaves, width),
-        out_shape=jax.ShapeDtypeStruct((128, leaves), f32),
-        in_specs=[smem, smem, smem, smem, vmem, vmem],
-        out_specs=vmem,
+        out_shape=(
+            jax.ShapeDtypeStruct((128, leaves), f32),
+            jax.ShapeDtypeStruct((shift.shape[1], shift.shape[0], shift.shape[2]), f32),
+        ),
+        in_specs=[smem, smem, smem, smem, vmem, vmem, pl.BlockSpec(memory_space=pl.ANY)],
+        out_specs=(vmem, pl.BlockSpec(memory_space=pl.ANY)),
         scratch_shapes=[
             pltpu.VMEM((leaves, 128, 48), bf16),
             pltpu.VMEM((leaves + 1, 128, 128), f32),
-            pltpu.VMEM((48, QUAD * 128), bf16),
-            pltpu.VMEM((48, QUAD * 128), bf16),
-            pltpu.VMEM((128, QUAD * 128), f32),
-            pltpu.VMEM((128, QUAD * 128), f32),
-        ],
+            pltpu.SemaphoreType.DMA((shift.shape[1],)),
+        ]
+        + [pltpu.VMEM((48, QUAD * 128), bf16)] * GROUP
+        + [pltpu.VMEM((128, QUAD * 128), f32)] * GROUP,
         compiler_params=pltpu.CompilerParams(vmem_limit_bytes=VMEM_LIMIT),
         cost_estimate=pl.CostEstimate(flops=pairs * 96, bytes_accessed=1 << 20, transcendentals=pairs),
         name="near",
-    )(counts, sources, offsets, total, data, table)
+    )(counts, sources, offsets, total, data, table, shift)
 
 
 def count_kernel(blocks, slot_ref, class_ref, out_ref, high, low, held):
@@ -266,27 +286,41 @@
 
 
 def far_kernel(
-    grands, ids_ref, lc_ref, pc_ref, cc_ref, own_ref, got_ref, pown_ref, pgot_ref, coarse_ref,
+    grands, caps, ids_ref, lc_ref, pc_ref, cc_ref, own_ref, pown_ref, got_ref,
     shift_ref, down_ref, pos_ref, chg_ref, self_ref, near_ref, out_ref,
     leaf_src, parent_src, coarse_src, total, wide, spread, held,
+    down, sems, parent_rows, lifted_rows,
 ):
     o = pl.program_id(0)
     leaves, coef = own_ref.shape
     parents = pown_ref.shape[0]
-    coarse = coarse_ref.shape[0]
+    coarse = coarse_src.shape[1]
+    devices = got_ref.shape[0]
+    cap_l, cap_p = caps
+    copies = [pltpu.make_async_copy(down_ref.at[:, c, :], down.at[c], sems.at[c]) for c in range(8)]
 
     @pl.when(o == 0)
     def _():
         total[...] = jnp.zeros_like(total)
+        for copy in copies:
+            copy.start()
         leaf_src[...] = jnp.zeros_like(leaf_src)
-        parent_src[...] = jnp.zeros_like(parent_src)
-        for target, first, second in ((leaf_src, own_ref, got_ref), (parent_src, pown_ref, pgot_ref)):
-            n = first.shape[0]
-            for side, half in enumerate(split2(first[...])):
-                target[side, :n, :] = half
-            for side, half in enumerate(split2(second[...])):
-                target[side, n : n + second.shape[0], :] = half
-        for side, half in enumerate(split2(coarse_ref[...])):
+        parent_rows[...] = jnp.zeros_like(parent_rows)
+        for side, half in enumerate(split2(own_ref[...])):
+            leaf_src[side, :leaves, :] = half
+        parent_rows[:parents, :] = pown_ref[...]
+
+        for d in range(devices):
+            got = got_ref[d]
+            first, second = leaves + d * cap_l, parents + d * cap_p
+            for side, half in enumerate(split2(got[:cap_l])):
+                leaf_src[side, first : first + cap_l, :] = half
+            parent_rows[second : second + cap_p, :] = got[cap_l : cap_l + cap_p]
+            lifted_rows[d * grands : (d + 1) * grands, :] = got[cap_l + cap_p : cap_l + cap_p + grands]
+        for side, half in enumerate(split2(parent_rows[...])):
+            parent_src[side] = half
+        sums = [jnp.sum(lifted_rows[8 * m : 8 * m + 8, :], axis=0, keepdims=True) for m in range(coarse)]
+        for side, half in enumerate(split2(jnp.concatenate(sums, axis=0))):
             coarse_src[side] = half
 
     def grouped(counts, source):
@@ -304,19 +338,21 @@
 
     @pl.when(o == pl.num_programs(0) - 1)
     def _():
+        for copy in copies:
+            copy.wait()
         far_parent = total[leaves : leaves + parents, :]
         far_coarse = total[leaves + parents :, :]
         rows = lax.broadcasted_iota(jnp.int32, (coarse, coef), 0)
         grand_rows = []
         for g in range(grands):
             mine = jnp.sum(jnp.where(rows == ids_ref[grands + g], far_coarse, 0.0), axis=0, keepdims=True)
-            grand_rows.append(dot_nt(mine, down_ref[ids_ref[g]]))
+            grand_rows.append(dot_nt(mine, down[ids_ref[g]]))
         grand = jnp.concatenate(grand_rows, axis=0)
         for c in range(8):
-            spread_to(spread, pl.ds(c, grands, stride=8), dot_nt(grand, down_ref[c]))
+            spread_to(spread, pl.ds(c, grands, stride=8), dot_nt(grand, down[c]))
         parent = joined(spread, slice(None), coef) + far_parent
         for c in range(8):
-            spread_to(wide, pl.ds(c, parents, stride=8), dot_nt(parent, down_ref[c]))
+            spread_to(wide, pl.ds(c, parents, stride=8), dot_nt(parent, down[c]))
         loc = joined(wide, slice(None), coef) + total[:leaves, :]
         spread_to(wide, slice(None), loc)
         for b in range(wide.shape[0]):
@@ -345,9 +381,9 @@
         out_ref[...] = (far + near_ref[...] - chg_ref[...].T * alone).T
 
 
-def far_call(ids, lc, pc, cc, own, got, pown, pgot, coarse, shift, down, pos, chg, alone, near):
+def far_call(caps, ids, lc, pc, cc, own, pown, got, shift, down, pos, chg, alone, near):
     operators, coef = shift.shape[:2]
-    leaves, parents, ncoarse = own.shape[0], pown.shape[0], coarse.shape[0]
+    leaves, parents, ncoarse = own.shape[0], pown.shape[0], cc.shape[1]
     vmem = pl.BlockSpec(memory_space=pltpu.VMEM)
     smem = pl.BlockSpec(memory_space=pltpu.SMEM)
     wide = pl.cdiv(coef, 128) * 128
@@ -356,12 +392,12 @@
         return pl.BlockSpec((1,) + x.shape[1:], lambda o: (o,) + (0,) * (x.ndim - 1))
 
     return pl.pallas_call(
-        functools.partial(far_kernel, parents // 8),
+        functools.partial(far_kernel, parents // 8, caps),
         grid=(operators,),
         out_shape=jax.ShapeDtypeStruct((leaves, 128), f32),
         in_specs=[
-            smem, per_operator(lc), per_operator(pc), per_operator(cc), vmem, vmem, vmem, vmem, vmem,
-            per_operator(shift), vmem, vmem, vmem, vmem, vmem,
+            smem, per_operator(lc), per_operator(pc), per_operator(cc), vmem, vmem, vmem,
+            per_operator(shift), pl.BlockSpec(memory_space=pl.ANY), vmem, vmem, vmem, vmem,
         ],
         out_specs=vmem,
         scratch_shapes=[
@@ -372,10 +408,14 @@
             pltpu.VMEM((wide // 128, leaves, 128), f32),
             pltpu.VMEM((wide // 128, parents, 128), f32),
             pltpu.VMEM((wide, leaves), f32),
+            pltpu.VMEM((8, coef, coef), f32),
+            pltpu.SemaphoreType.DMA((8,)),
+            pltpu.VMEM((pc.shape[1] * 128, coef), f32),
+            pltpu.VMEM((8 * ncoarse, coef), f32),
         ],
         compiler_params=pltpu.CompilerParams(vmem_limit_bytes=VMEM_LIMIT),
         name="far",
-    )(ids, lc, pc, cc, own, got, pown, pgot, coarse, shift, down, pos, chg, alone, near)
+    )(ids, lc, pc, cc, own, pown, got, shift, down, pos, chg, alone, near)
 
 
 def per_device(
@@ -412,14 +452,17 @@
     before = lax.ppermute(data[leaves - RIM :], AXES, up)
     after = lax.ppermute(data[:RIM], AXES, down)
 
-    leaf_rows, parent_rows, lifted = upward_call(ids, pos, chg, up_shift)
-
-    outgoing = jnp.concatenate([leaf_rows[asked[:, :cap_l]], parent_rows[asked[:, cap_l:]]], axis=1)
+    leaf_rows, parent_rows, lifted = upward_call(ids, pos, chg, jnp.swapaxes(up_shift, 0, 1))
+
+    outgoing = jnp.concatenate(
+        [
+            leaf_rows[asked[:, :cap_l]],
+            parent_rows[asked[:, cap_l:]],
+            jnp.broadcast_to(lifted[None], (devices,) + lifted.shape),
+        ],
+        axis=1,
+    )
     arrived = lax.all_to_all(outgoing, AXES, split_axis=0, concat_axis=0, tiled=True)
-    member = (
-        jnp.arange(ncoarse, dtype=jnp.int32)[:, None] == grand_ids[None, :] // 8
-    ).astype(f32)
-    coarse = lax.psum(jnp.sum(member[:, :, None] * lifted[None], axis=1), AXES)
 
     extended = jnp.concatenate([before, data, after, jnp.zeros((1, 8, size), f32)], axis=0)
     present = near_leaves >= 0
@@ -433,7 +476,9 @@
     classes = jnp.arange(27, dtype=jnp.int32)
     shifts = jnp.stack([classes // 9 - 1, classes // 3 % 3 - 1, classes % 3 - 1], axis=1).astype(f32)
     table = jnp.broadcast_to(jnp.pad(shifts, ((0, 0), (0, 5)))[:, :, None], (27, 8, size))
-    near = near_call(counts, source, offset, total, extended, table, leaves, padded)
+    near, shifts_by_class = near_call(
+        counts, source, offset, total, extended, table, jnp.swapaxes(far_shift, 0, 1), leaves, padded
+    )
     target_ids = first + jnp.arange(leaves, dtype=jnp.int32)
     alone = jnp.sum(
         ((near_leaves == target_ids[:, None]) & (near_offsets == 13)).astype(f32), axis=1
@@ -447,8 +492,8 @@
     where = coarse_lists[:, :, None] == jnp.arange(ncoarse, dtype=jnp.int32)
     cc = jnp.sum((hit[..., None] & where[None]).astype(f32), axis=2)
     out = far_call(
-        ids, lc, pc, cc, leaf_rows, arrived[:, :cap_l].reshape(-1, coef), parent_rows,
-        arrived[:, cap_l:].reshape(-1, coef), coarse, far_shift, down_shift, pos, chg, alone, near,
+        (cap_l, cap_p), ids, lc, pc, cc, leaf_rows, parent_rows, arrived, shifts_by_class,
+        jnp.swapaxes(down_shift, 0, 1), pos, chg, alone, near,
     )
     return out.reshape(-1)
 

time: 229 us -> 304 us (1.33)
  Pallas kernels: 130 us -> 265 us
  blocking collectives: 40.4 us -> 0 us
  local copies, waits for them, and re-layouts: 31.3 us -> 13.5 us
    pallas_call x2, Pallas kernels: 104 us -> 240 us  [the longest x1 217 us: near_call(): pl.pallas_call(functools.partial(near_kernel, leaves, width), out_shape=(...]
    psum x1 -> x0, blocking collectives: 40.4 us -> none  [per_device(): coarse = lax.psum(jnp.sum(member[:, :, None] * lifted[None], axis=1), AXES)]
    unnamed x26 -> x27, local copies, waits for them, and re-layouts: 21.5 us -> 5.39 us
  transfers between devices with their start and end apart: 4 -> 4, of which waited for: 0 -> 0; matrix products, arithmetic and copies ran while one was open for 15% -> 5% of each run, Pallas kernels for 47% -> 80%
where the time goes in v2:
time: 304 us; the launch traced here: 303 us
  Pallas kernels  265 us (87%)
  starting transfers between devices  18.7 us (6%)
  local copies, waits for them, and re-layouts  13.5 us (4%)
  other arithmetic  4.77 us (2%)
    pallas_call x1, Pallas kernels, near_call(): pl.pallas_call(functools.partial(near_kernel, leaves, width), out_shape=(...  217 us
    pallas_call x1, Pallas kernels, far_call(): pl.pallas_call(functools.partial(far_kernel, parents // 8, caps), grid=(o...  23.8 us
    pallas_call x2, Pallas kernels, count_call(): pl.pallas_call(functools.partial(count_kernel, blocks), out_shape=jax.Sha...  14.6 us
    pallas_call x1, Pallas kernels, upward_call(): pl.pallas_call(upward_kernel, out_shape=(jax.ShapeDtypeStruct((leaves, co...  10.4 us
    all_to_all x1, starting transfers between devices, per_device(): lax.all_to_all(outgoing, AXES, split_axis=0, concat_axis=0, tiled=True)  7.94 us
    all_to_all x1, starting transfers between devices, per_device(): lax.all_to_all(jnp.concatenate([leaf_plan, parent_plan], 2), AXES, split_...  7.32 us
  transfers between devices with their start and end apart: 4, of which 0 were waited for; matrix products, arithmetic and copies ran while one was open for 5% of the time, Pallas kernels for 80%

profile of v2, /device:TPU:0, one launch (start us, length us, event | category | flops | bytes accessed | tf_op | source)
XLA Modules:
  0.0 303.0 jit_solution(10913357563741966386)
XLA Ops:
  0.0 0.8 pad_add_fusion
  0.8 0.7 copy.44
  1.5 7.3 %all-to-all-start = ((s32[1,32,20]{2,0,1:T(1,128)}), s32[1,32,20]{2,0,1:T(1,128)S(1)}, u32[]{:S(2)}, u32[]{:S(2)}) async-start(s32[1,32,20]{2,0,1:T(1,128)} %copy.44), calls=%async_computation | async-start | bytes 32768 | tf_op jit(solution)/shard_map/all_to_all | solution.py:441
  8.8 1.7 bitcast_dynamic-update-slice_fusion
  10.4 0.8 bitcast_dynamic-update-slice_fusion.1
  11.3 2.2 collective-permute-start
  13.5 1.3 collective-permute-start.1
  14.9 1.2 fusion
  16.1 0.6 pad_add_fusion.1.ids_ref
  16.7 0.8 copy.42.slot_ref
  17.4 0.7 copy.43.class_ref
  18.2 10.4 %upward.1 = (f32[128,286]{1,0:T(8,128)}, f32[16,286]{1,0:T(8,128)}, f32[2,286]{1,0:T(2,128)}) custom-call(s32[4]{0:T(128)} %pad_add_fusion.1.ids_ref, f32[3,128,128]{2,1,0:T(8,128)} %get-tuple-element.16.pos_ref, f32[128,128]{1,0:T(8,128)} %bitcast.24, f32[286,8,286]{2,1,0:T(8,128)} %bitcast.22), custom_call_target="tpu_custom_call" | custom-call | tf_op jit(solution)/shard_map/upward/pallas_call | solution.py:109
  28.8 0.1 reshape.157
  28.9 1.6 gather_fusion.1
  30.6 1.6 gather_fusion
  32.3 1.2 pad_maximum_fusion
  33.4 7.9 %all-to-all-start.1 = ((f32[32,22,286]{2,1,0:T(8,128)}), f32[32,22,286]{2,1,0:T(8,128)S(1)}, u32[]{:S(2)}, u32[]{:S(2)}) async-start(f32[32,22,286]{2,1,0:T(8,128)} %pad_maximum_fusion), calls=%async_computation.1 | async-start | bytes 2359296 | tf_op jit(solution)/shard_map/all_to_all | solution.py:465
  41.6 0.1 convert_reduce_fusion
  41.7 12.4 %count.2 = bf16[10240,128]{1,0:T(8,128)(2,1)} custom-call(s32[128,189]{1,0:T(8,128)} %copy.42.slot_ref, s32[128,189]{1,0:T(8,128)} %copy.43.class_ref), custom_call_target="tpu_custom_call" | custom-call | flops 671088640 | bytes 2621440 | tf_op jit(solution)/shard_map/count/pallas_call | solution.py:269
  54.1 0.1 copy.50
  54.2 0.7 reshape.144.src_ref
  54.9 0.1 copy.51
  55.0 0.7 reshape.145.off_ref
  55.8 0.7 copy.49.cc_ref
  56.6 2.2 count.3
  58.9 0.5 convert_reduce_fusion.1
  59.4 0.1 maximum_maximum_fusion
  59.5 1.0 copy.48.data_ref
  60.5 0.7 broadcast_in_dim.52.table_ref
  61.3 216.6 %near.1 = (f32[128,128]{1,0:T(8,128)}, f32[16,286,286]{2,1,0:T(8,128)}) custom-call(s32[129]{0:T(256)} %get-tuple-element.23.count_ref, s32[3612]{0:T(1024)} %reshape.144.src_ref, s32[3612]{0:T(1024)} %reshape.145.off_ref, s32[1]{0:T(128)} %bitcast.6.total_ref, f32[193,8,128]{2,1,0:T(8,128)} %copy.48.data_ref, f32[27,8,128]{2,1,0:T(8,128)} %broadcast_in_dim.52.table_ref, ...), custom_call_target="tpu_custom_call" | custom-call | flops 3623878656 | bytes 1048576 | tf_op jit(solution)/shard_map/near/pallas_call | solution.py:225
  277.9 1.0 copy-done.1
  279.0 23.8 %far.1 = f32[128,128]{1,0:T(8,128)} custom-call(s32[4]{0:T(128)} %pad_add_fusion.1.ids_ref, bf16[16,5,128,128]{3,2,1,0:T(8,128)(2,1)} %bitcast.20, bf16[16,2,16,128]{3,2,1,0:T(8,128)(2,1)} %bitcast.26, f32[16,8,8]{2,1,0:T(8,128)} %copy.49.cc_ref, f32[128,286]{1,0:T(8,128)} %get-tuple-element.10.own_ref, f32[16,286]{1,0:T(8,128)} %get-tuple-element.11.pown_ref, ...), custom_call_target="tpu_custom_call" | custom-call | tf_op jit(solution)/shard_map/far/pallas_call | solution.py:394
  (45 shorter events, 0.8 us)
Async XLA Ops:
  0.0 14.9 %copy-start.5 = (s32[128,27]{0,1:T(8,128)S(1)}, s32[128,27]{0,1:T(8,128)}, u32[]{:S(2)}) copy-start(s32[128,27]{0,1:T(8,128)} %param.17) | copy-start | bytes 41476
  0.0 14.9 %copy-start.4 = (s32[128,27]{0,1:T(8,128)S(1)}, s32[128,27]{0,1:T(8,128)}, u32[]{:S(2)}) copy-start(s32[128,27]{0,1:T(8,128)} %param.18) | copy-start | bytes 41476
  0.0 16.7 %copy-start.2 = (s32[128,189]{0,1:T(8,128)S(1)}, s32[128,189]{0,1:T(8,128)}, u32[]{:S(2)}) copy-start(s32[128,189]{0,1:T(8,128)} %param.19) | copy-start | bytes 290308
  0.0 17.4 %copy-start.3 = (s32[128,189]{0,1:T(8,128)S(1)}, s32[128,189]{0,1:T(8,128)}, u32[]{:S(2)}) copy-start(s32[128,189]{0,1:T(8,128)} %param.20) | copy-start | bytes 290308
  1.5 27.2 %all-to-all-start = ((s32[1,32,20]{2,0,1:T(1,128)}), s32[1,32,20]{2,0,1:T(1,128)S(1)}, u32[]{:S(2)}, u32[]{:S(2)}) async-start(s32[1,32,20]{2,0,1:T(1,128)} %copy.44), calls=%async_computation | async-start | bytes 32768 | tf_op jit(solution)/shard_map/all_to_all | solution.py:441
  11.3 48.0 %collective-permute-start = (f32[32,8,128]{2,0,1:T(8,128)S(1)}, f32[32,8,128]{2,0,1:T(8,128)S(1)}, u32[]{:S(2)}, u32[]{:S(2)}) collective-permute-start(f32[32,8,128]{2,0,1:T(8,128)S(1)} %get-tuple-element.17), channel_id=1, source_target_pairs={{0,1},{1,2},{2,3},{3,4},{4,5},{5,6},{6,7},{7,8},{8,9},{9,10},{10,1... | collective-permute-start | bytes 393224 | tf_op jit(solution)/shard_map/ppermute | solution.py:452
  13.5 45.9 %collective-permute-start.1 = (f32[32,8,128]{2,0,1:T(8,128)S(1)}, f32[32,8,128]{2,0,1:T(8,128)S(1)}, u32[]{:S(2)}, u32[]{:S(2)}) collective-permute-start(f32[32,8,128]{2,0,1:T(8,128)S(1)} %get-tuple-element.18), channel_id=1, source_target_pairs={{1,0},{2,1},{3,2},{4,3},{5,4},{6,5},{7,6},{8,7},{9,8},{10,9},{11,1... | collective-permute-start | bytes 393224 | tf_op jit(solution)/shard_map/ppermute | solution.py:453
  28.6 2.0 copy-start
  30.6 1.6 copy-start.8
  33.4 8.0 %copy-start.6 = (s32[8,7]{1,0:T(8,128)S(1)}, s32[8,7]{1,0:T(8,128)}, u32[]{:S(2)}) copy-start(s32[8,7]{1,0:T(8,128)} %param.25) | copy-start | bytes 676
  33.4 8.1 %copy-start.7 = (s32[8,7]{1,0:T(8,128)S(1)}, s32[8,7]{1,0:T(8,128)}, u32[]{:S(2)}) copy-start(s32[8,7]{1,0:T(8,128)} %param.26) | copy-start | bytes 676
  33.4 244.5 %all-to-all-start.1 = ((f32[32,22,286]{2,1,0:T(8,128)}), f32[32,22,286]{2,1,0:T(8,128)S(1)}, u32[]{:S(2)}, u32[]{:S(2)}) async-start(f32[32,22,286]{2,1,0:T(8,128)} %pad_maximum_fusion), calls=%async_computation.1 | async-start | bytes 2359296 | tf_op jit(solution)/shard_map/all_to_all | solution.py:465
  277.9 1.0 copy-start.1

commit v3 on v2

--- a/solution.py
+++ b/solution.py
@@ -128,16 +128,10 @@
 
 
 def near_kernel(
-    leaves, width, count_ref, src_ref, off_ref, total_ref, data_ref, table_ref, shift_ref, out_ref, order_ref,
-    targets, acc, sems, *held,
+    leaves, width, count_ref, src_ref, off_ref, total_ref, data_ref, table_ref, out_ref,
+    targets, acc, *held,
 ):
     bs, rs = held[:GROUP], held[GROUP:]
-    copies = [
-        pltpu.make_async_copy(shift_ref.at[:, o, :], order_ref.at[o], sems.at[o])
-        for o in range(shift_ref.shape[1])
-    ]
-    for copy in copies:
-        copy.start()
     row = lax.broadcasted_iota(jnp.int32, (8, 128), 0)
     soft = softening * softening
 
@@ -214,41 +208,39 @@
         return carry
 
     lax.fori_loop(0, leaves // 8, finish, 0)
-    for copy in copies:
-        copy.wait()
-
-
-def near_call(counts, sources, offsets, total, data, table, shift, leaves, width):
+
+
+def near_call(counts, sources, offsets, total, data, table, leaves, width):
     vmem = pl.BlockSpec(memory_space=pltpu.VMEM)
     smem = pl.BlockSpec(memory_space=pltpu.SMEM)
     pairs = leaves * 18 * 128 * 128
     return pl.pallas_call(
         functools.partial(near_kernel, leaves, width),
-        out_shape=(
-            jax.ShapeDtypeStruct((128, leaves), f32),
-            jax.ShapeDtypeStruct((shift.shape[1], shift.shape[0], shift.shape[2]), f32),
-        ),
-        in_specs=[smem, smem, smem, smem, vmem, vmem, pl.BlockSpec(memory_space=pl.ANY)],
-        out_specs=(vmem, pl.BlockSpec(memory_space=pl.ANY)),
+        out_shape=jax.ShapeDtypeStruct((128, leaves), f32),
+        in_specs=[smem, smem, smem, smem, vmem, vmem],
+        out_specs=vmem,
         scratch_shapes=[
             pltpu.VMEM((leaves, 128, 48), bf16),
             pltpu.VMEM((leaves + 1, 128, 128), f32),
-            pltpu.SemaphoreType.DMA((shift.shape[1],)),
         ]
         + [pltpu.VMEM((48, QUAD * 128), bf16)] * GROUP
         + [pltpu.VMEM((128, QUAD * 128), f32)] * GROUP,
         compiler_params=pltpu.CompilerParams(vmem_limit_bytes=VMEM_LIMIT),
         cost_estimate=pl.CostEstimate(flops=pairs * 96, bytes_accessed=1 << 20, transcendentals=pairs),
         name="near",
-    )(counts, sources, offsets, total, data, table, shift)
-
-
-def count_kernel(blocks, slot_ref, class_ref, out_ref, high, low, held):
-    targets, width = slot_ref.shape
+    )(counts, sources, offsets, total, data, table)
+
+
+def count_kernel(blocks, slot_ref, class_ref, out_ref, turned, high, low, held):
+    filled, targets = slot_ref.shape
+    width = high.shape[1]
     heights = held.shape[0] // targets
     slots = slot_ref[...]
-    high[...] = jnp.where(slots >= 0, class_ref[...] * blocks + slots // 128, -1)
-    low[...] = jnp.where(slots >= 0, slots % 128, -1)
+    turned[...] = jnp.full(turned.shape, -1.0, f32)
+    turned[:filled, :targets] = jnp.where(slots >= 0, class_ref[...] * blocks + slots // 128, -1).astype(f32)
+    high[...] = turned[...].T.astype(jnp.int32)
+    turned[:filled, :targets] = jnp.where(slots >= 0, slots % 128, -1).astype(f32)
+    low[...] = turned[...].T.astype(jnp.int32)
     high_row = lax.broadcasted_iota(jnp.int32, (heights, width), 0)
     low_row = lax.broadcasted_iota(jnp.int32, (128, width), 0)
 
@@ -258,12 +250,13 @@
         held[pl.ds(t, heights, stride=targets), :] = lax.dot_general(h, w, NT, preferred_element_type=f32)
         return carry
 
-    lax.fori_loop(0, targets, one, 0, unroll=4)
+    lax.fori_loop(0, targets, one, 0, unroll=8)
     out_ref[...] = held[...].astype(bf16)
 
 
 def count_call(slots, classes, blocks, operators):
-    targets, width = slots.shape
+    filled, targets = slots.shape
+    width = pl.cdiv(filled, 128) * 128
     vmem = pl.BlockSpec(memory_space=pltpu.VMEM)
     rows = operators * blocks * targets
     held = pl.pallas_call(
@@ -272,8 +265,9 @@
         in_specs=[vmem, vmem],
         out_specs=vmem,
         scratch_shapes=[
-            pltpu.VMEM((targets, width), jnp.int32),
-            pltpu.VMEM((targets, width), jnp.int32),
+            pltpu.VMEM((width, 128), f32),
+            pltpu.VMEM((128, width), jnp.int32),
+            pltpu.VMEM((128, width), jnp.int32),
             pltpu.VMEM((rows, 128), f32),
         ],
         compiler_params=pltpu.CompilerParams(vmem_limit_bytes=VMEM_LIMIT),
@@ -289,7 +283,7 @@
     grands, caps, ids_ref, lc_ref, pc_ref, cc_ref, own_ref, pown_ref, got_ref,
     shift_ref, down_ref, pos_ref, chg_ref, self_ref, near_ref, out_ref,
     leaf_src, parent_src, coarse_src, total, wide, spread, held,
-    down, sems, parent_rows, lifted_rows,
+    down, sems, parent_rows, lifted_rows, shifts, shift_sems,
 ):
     o = pl.program_id(0)
     leaves, coef = own_ref.shape
@@ -297,12 +291,16 @@
     coarse = coarse_src.shape[1]
     devices = got_ref.shape[0]
     cap_l, cap_p = caps
+    operators = shifts.shape[0]
+    moves = [
+        pltpu.make_async_copy(shift_ref.at[:, i, :], shifts.at[i], shift_sems.at[i]) for i in range(operators)
+    ]
     copies = [pltpu.make_async_copy(down_ref.at[:, c, :], down.at[c], sems.at[c]) for c in range(8)]
 
     @pl.when(o == 0)
     def _():
         total[...] = jnp.zeros_like(total)
-        for copy in copies:
+        for copy in moves + copies:
             copy.start()
         leaf_src[...] = jnp.zeros_like(leaf_src)
         parent_rows[...] = jnp.zeros_like(parent_rows)
@@ -334,7 +332,13 @@
         few, coarse_src[1], preferred_element_type=f32
     )
     stacked = jnp.concatenate([grouped(lc_ref, leaf_src), grouped(pc_ref, parent_src), small], axis=0)
-    total[...] += dot_nt(stacked, shift_ref[0])
+    for i in range(operators):
+
+        @pl.when(o == i)
+        def _(i=i):
+            moves[i].wait()
+
+    total[...] += dot_nt(stacked, shifts[o])
 
     @pl.when(o == pl.num_programs(0) - 1)
     def _():
@@ -382,7 +386,7 @@
 
 
 def far_call(caps, ids, lc, pc, cc, own, pown, got, shift, down, pos, chg, alone, near):
-    operators, coef = shift.shape[:2]
+    coef, operators = shift.shape[:2]
     leaves, parents, ncoarse = own.shape[0], pown.shape[0], cc.shape[1]
     vmem = pl.BlockSpec(memory_space=pltpu.VMEM)
     smem = pl.BlockSpec(memory_space=pltpu.SMEM)
@@ -397,7 +401,7 @@
         out_shape=jax.ShapeDtypeStruct((leaves, 128), f32),
         in_specs=[
             smem, per_operator(lc), per_operator(pc), per_operator(cc), vmem, vmem, vmem,
-            per_operator(shift), pl.BlockSpec(memory_space=pl.ANY), vmem, vmem, vmem, vmem,
+            pl.BlockSpec(memory_space=pl.ANY), pl.BlockSpec(memory_space=pl.ANY), vmem, vmem, vmem, vmem,
         ],
         out_specs=vmem,
         scratch_shapes=[
@@ -412,6 +416,8 @@
             pltpu.SemaphoreType.DMA((8,)),
             pltpu.VMEM((pc.shape[1] * 128, coef), f32),
             pltpu.VMEM((8 * ncoarse, coef), f32),
+            pltpu.VMEM((operators, coef, coef), f32),
+            pltpu.SemaphoreType.DMA((operators,)),
         ],
         compiler_params=pltpu.CompilerParams(vmem_limit_bytes=VMEM_LIMIT),
         name="far",
@@ -476,9 +482,7 @@
     classes = jnp.arange(27, dtype=jnp.int32)
     shifts = jnp.stack([classes // 9 - 1, classes // 3 % 3 - 1, classes % 3 - 1], axis=1).astype(f32)
     table = jnp.broadcast_to(jnp.pad(shifts, ((0, 0), (0, 5)))[:, :, None], (27, 8, size))
-    near, shifts_by_class = near_call(
-        counts, source, offset, total, extended, table, jnp.swapaxes(far_shift, 0, 1), leaves, padded
-    )
+    near = near_call(counts, source, offset, total, extended, table, leaves, padded)
     target_ids = first + jnp.arange(leaves, dtype=jnp.int32)
     alone = jnp.sum(
         ((near_leaves == target_ids[:, None]) & (near_offsets == 13)).astype(f32), axis=1
@@ -486,13 +490,13 @@
 
     leaf_blocks = pl.cdiv(leaves + devices * cap_l, 128)
     parent_blocks = pl.cdiv(parents + devices * cap_p, 128)
-    lc = count_call(far_leaves, far_leaf_class, leaf_blocks, operators)
-    pc = count_call(far_parents, far_parent_class, parent_blocks, operators)
+    lc = count_call(far_leaves.T, far_leaf_class.T, leaf_blocks, operators)
+    pc = count_call(far_parents.T, far_parent_class.T, parent_blocks, operators)
     hit = coarse_class[None] == jnp.arange(operators, dtype=jnp.int32)[:, None, None]
     where = coarse_lists[:, :, None] == jnp.arange(ncoarse, dtype=jnp.int32)
     cc = jnp.sum((hit[..., None] & where[None]).astype(f32), axis=2)
     out = far_call(
-        (cap_l, cap_p), ids, lc, pc, cc, leaf_rows, parent_rows, arrived, shifts_by_class,
+        (cap_l, cap_p), ids, lc, pc, cc, leaf_rows, parent_rows, arrived, jnp.swapaxes(far_shift, 0, 1),
         jnp.swapaxes(down_shift, 0, 1), pos, chg, alone, near,
     )
     return out.reshape(-1)

time: 304 us -> 148 us (0.49)
  Pallas kernels: 265 us -> 109 us
    pallas_call x1, Pallas kernels: 217 us -> 59.9 us  [near_call(): pl.pallas_call(functools.partial(near_kernel, leaves, width), out_shape=j...]
  transfers between devices with their start and end apart: 4 -> 4, of which waited for: 0 -> 0; matrix products, arithmetic and copies ran while one was open for 5% -> 11% of each run, Pallas kernels for 80% -> 57%
where the time goes in v3:
time: 148 us; the launch traced here: 146 us
  Pallas kernels  109 us (74%)
  starting transfers between devices  18.7 us (13%)
  local copies, waits for them, and re-layouts  13.5 us (9%)
  other arithmetic  4.92 us (3%)
    pallas_call x1, Pallas kernels, near_call(): pl.pallas_call(functools.partial(near_kernel, leaves, width), out_shape=j...  59.9 us
    pallas_call x1, Pallas kernels, far_call(): pl.pallas_call(functools.partial(far_kernel, parents // 8, caps), grid=(o...  25.3 us
    pallas_call x2, Pallas kernels, count_call(): pl.pallas_call(functools.partial(count_kernel, blocks), out_shape=jax.Sha...  13.1 us
    pallas_call x1, Pallas kernels, upward_call(): pl.pallas_call(upward_kernel, out_shape=(jax.ShapeDtypeStruct((leaves, co...  10.4 us
    all_to_all x1, starting transfers between devices, per_device(): lax.all_to_all(outgoing, AXES, split_axis=0, concat_axis=0, tiled=True)  7.94 us
    all_to_all x1, starting transfers between devices, per_device(): lax.all_to_all(jnp.concatenate([leaf_plan, parent_plan], 2), AXES, split_...  7.3 us
    unnamed x27, local copies, waits for them, and re-layouts  5.35 us
  transfers between devices with their start and end apart: 4, of which 0 were waited for; matrix products, arithmetic and copies ran while one was open for 11% of the time, Pallas kernels for 57%

profile of v3, /device:TPU:0, one launch (start us, length us, event | category | flops | bytes accessed | tf_op | source)
XLA Modules:
  0.0 146.3 jit_solution(5567288288147629438)
XLA Ops:
  0.0 0.7 pad_add_fusion
  0.7 0.7 copy.44
  1.4 7.3 %all-to-all-start = ((s32[1,32,20]{2,0,1:T(1,128)}), s32[1,32,20]{2,0,1:T(1,128)S(1)}, u32[]{:S(2)}, u32[]{:S(2)}) async-start(s32[1,32,20]{2,0,1:T(1,128)} %copy.44), calls=%async_computation | async-start | bytes 32768 | tf_op jit(solution)/shard_map/all_to_all | solution.py:447
  8.7 1.7 %bitcast_dynamic-update-slice_fusion = (f32[128,8,128]{2,0,1:T(8,128)S(1)}, f32[3,128,128]{2,1,0:T(8,128)}) fusion(f32[1,3,128,128]{3,1,2,0:T(4,128)} %bitcast.34), kind=kLoop, calls=%fused_computation.6 | loop fusion | bytes 589824
  10.4 0.8 bitcast_dynamic-update-slice_fusion.1
  11.3 2.2 %collective-permute-start = (f32[32,8,128]{2,0,1:T(8,128)S(1)}, f32[32,8,128]{2,0,1:T(8,128)S(1)}, u32[]{:S(2)}, u32[]{:S(2)}) collective-permute-start(f32[32,8,128]{2,0,1:T(8,128)S(1)} %get-tuple-element.13), channel_id=1, source_target_pairs={{0,1},{1,2},{2,3},{3,4},{4,5},{5,6},{6,7},{7,8},{8,9},{9,10},{10,1... | collective-permute-start | bytes 393224 | tf_op jit(solution)/shard_map/ppermute | solution.py:458
  13.5 1.3 collective-permute-start.1
  14.9 1.2 fusion
  16.0 0.7 pad_add_fusion.1.ids_ref
  16.7 10.4 %upward.1 = (f32[128,286]{1,0:T(8,128)}, f32[16,286]{1,0:T(8,128)}, f32[2,286]{1,0:T(2,128)}) custom-call(s32[4]{0:T(128)} %pad_add_fusion.1.ids_ref, f32[3,128,128]{2,1,0:T(8,128)} %get-tuple-element.12.pos_ref, f32[128,128]{1,0:T(8,128)} %bitcast.29, f32[286,8,286]{2,1,0:T(8,128)} %bitcast.27), custom_call_target="tpu_custom_call" | custom-call | tf_op jit(solution)/shard_map/upward/pallas_call | solution.py:109
  27.3 0.1 reshape.157
  27.5 1.6 %gather_fusion.1 = f32[128,286]{1,0:T(8,128)S(1)} fusion(f32[16,286]{1,0:T(8,128)} %get-tuple-element.9.pown_ref, s32[1024]{0:T(1024)S(1)} %get-tuple-element.22), kind=kCustom, calls=%fused_computation.1 | custom fusion | bytes 293376 | tf_op jit(solution)/shard_map/gather | solution.py:466
  29.1 1.6 %gather_fusion = f32[512,286]{1,0:T(8,128)S(1)} fusion(f32[128,286]{1,0:T(8,128)S(1)} %copy-done, s32[1024]{0:T(1024)S(1)} %get-tuple-element.23), kind=kCustom, calls=%fused_computation | custom fusion | bytes 1173504 | tf_op jit(solution)/shard_map/gather | solution.py:465
  30.8 1.1 pad_maximum_fusion
  31.9 7.9 %all-to-all-start.1 = ((f32[32,22,286]{2,1,0:T(8,128)}), f32[32,22,286]{2,1,0:T(8,128)S(1)}, u32[]{:S(2)}, u32[]{:S(2)}) async-start(f32[32,22,286]{2,1,0:T(8,128)} %pad_maximum_fusion), calls=%async_computation.1 | async-start | bytes 2359296 | tf_op jit(solution)/shard_map/all_to_all | solution.py:471
  40.1 0.1 convert_reduce_fusion
  40.2 10.7 %count.2 = bf16[10240,128]{1,0:T(8,128)(2,1)} custom-call(s32[189,128]{1,0:T(8,128)} %bitcast.37, s32[189,128]{1,0:T(8,128)} %bitcast.38), custom_call_target="tpu_custom_call" | custom-call | flops 671088640 | bytes 2621440 | tf_op jit(solution)/shard_map/count/pallas_call | solution.py:262
  51.0 0.7 copy.49.cc_ref
  51.7 0.1 copy.51
  51.8 0.7 reshape.145.off_ref
  52.5 0.1 copy.50
  52.7 0.7 reshape.144.src_ref
  53.4 0.7 copy.42
  54.1 0.7 copy.43
  54.9 2.4 %count.3 = bf16[512,128]{1,0:T(8,128)(2,1)} custom-call(s32[189,16]{1,0:T(8,128)} %bitcast.32, s32[189,16]{1,0:T(8,128)} %bitcast.33), custom_call_target="tpu_custom_call" | custom-call | flops 33554432 | bytes 131072 | tf_op jit(solution)/shard_map/count/pallas_call | solution.py:262
  57.4 0.6 convert_reduce_fusion.2
  58.0 0.1 maximum_maximum_fusion
  58.1 1.0 copy.48.data_ref
  59.2 0.7 broadcast_in_dim.50.table_ref
  59.9 59.9 %near.1.near_ref = f32[128,128]{1,0:T(8,128)} custom-call(s32[129]{0:T(256)} %get-tuple-element.19.count_ref, s32[3612]{0:T(1024)} %reshape.144.src_ref, s32[3612]{0:T(1024)} %reshape.145.off_ref, s32[1]{0:T(128)} %bitcast.13.total_ref, f32[193,8,128]{2,1,0:T(8,128)} %copy.48.data_ref, f32[27,8,128]{2,1,0:T(8,128)} %broadcast_in_dim.50.table_ref), custom_call_target="tpu_custom_call" | custom-call | flops 3623878656 | bytes 1048576 | tf_op jit(solution)/shard_map/near/pallas_call | solution.py:217
  119.8 1.0 copy-done.1
  120.8 25.3 %far.1 = f32[128,128]{1,0:T(8,128)} custom-call(s32[4]{0:T(128)} %pad_add_fusion.1.ids_ref, bf16[16,5,128,128]{3,2,1,0:T(8,128)(2,1)} %bitcast.24, bf16[16,2,16,128]{3,2,1,0:T(8,128)(2,1)} %bitcast.31, f32[16,8,8]{2,1,0:T(8,128)} %copy.49.cc_ref, f32[128,286]{1,0:T(8,128)} %get-tuple-element.8.own_ref, f32[16,286]{1,0:T(8,128)} %get-tuple-element.9.pown_ref, ...), custom_call_target="tpu_custom_call" | custom-call | tf_op jit(solution)/shard_map/far/pallas_call | solution.py:398
  (45 shorter events, 0.8 us)
Async XLA Ops:
  0.0 14.8 %copy-start.2 = (s32[128,27]{0,1:T(8,128)S(1)}, s32[128,27]{0,1:T(8,128)}, u32[]{:S(2)}) copy-start(s32[128,27]{0,1:T(8,128)} %param.18) | copy-start | bytes 41476
  0.0 14.8 %copy-start.3 = (s32[128,27]{0,1:T(8,128)S(1)}, s32[128,27]{0,1:T(8,128)}, u32[]{:S(2)}) copy-start(s32[128,27]{0,1:T(8,128)} %param.17) | copy-start | bytes 41476
  1.4 25.7 %all-to-all-start = ((s32[1,32,20]{2,0,1:T(1,128)}), s32[1,32,20]{2,0,1:T(1,128)S(1)}, u32[]{:S(2)}, u32[]{:S(2)}) async-start(s32[1,32,20]{2,0,1:T(1,128)} %copy.44), calls=%async_computation | async-start | bytes 32768 | tf_op jit(solution)/shard_map/all_to_all | solution.py:447
  11.3 46.7 %collective-permute-start = (f32[32,8,128]{2,0,1:T(8,128)S(1)}, f32[32,8,128]{2,0,1:T(8,128)S(1)}, u32[]{:S(2)}, u32[]{:S(2)}) collective-permute-start(f32[32,8,128]{2,0,1:T(8,128)S(1)} %get-tuple-element.13), channel_id=1, source_target_pairs={{0,1},{1,2},{2,3},{3,4},{4,5},{5,6},{6,7},{7,8},{8,9},{9,10},{10,1... | collective-permute-start | bytes 393224 | tf_op jit(solution)/shard_map/ppermute | solution.py:458
  13.5 44.5 %collective-permute-start.1 = (f32[32,8,128]{2,0,1:T(8,128)S(1)}, f32[32,8,128]{2,0,1:T(8,128)S(1)}, u32[]{:S(2)}, u32[]{:S(2)}) collective-permute-start(f32[32,8,128]{2,0,1:T(8,128)S(1)} %get-tuple-element.14), channel_id=1, source_target_pairs={{1,0},{2,1},{3,2},{4,3},{5,4},{6,5},{7,6},{8,7},{9,8},{10,9},{11,1... | collective-permute-start | bytes 393224 | tf_op jit(solution)/shard_map/ppermute | solution.py:459
  27.1 2.0 %copy-start = (f32[128,286]{1,0:T(8,128)S(1)}, f32[128,286]{1,0:T(8,128)}, u32[]{:S(2)}) copy-start(f32[128,286]{1,0:T(8,128)} %get-tuple-element.8.own_ref) | copy-start | bytes 439300
  29.1 1.6 %copy-start.8 = (f32[2,286]{1,0:T(2,128)S(1)}, f32[2,286]{1,0:T(2,128)}, u32[]{:S(2)}) copy-start(f32[2,286]{1,0:T(2,128)} %get-tuple-element.10) | copy-start | bytes 6868
  31.9 8.0 %copy-start.6 = (s32[8,7]{1,0:T(8,128)S(1)}, s32[8,7]{1,0:T(8,128)}, u32[]{:S(2)}) copy-start(s32[8,7]{1,0:T(8,128)} %param.25) | copy-start | bytes 676
  31.9 8.1 %copy-start.7 = (s32[8,7]{1,0:T(8,128)S(1)}, s32[8,7]{1,0:T(8,128)}, u32[]{:S(2)}) copy-start(s32[8,7]{1,0:T(8,128)} %param.26) | copy-start | bytes 676
  31.9 87.8 %all-to-all-start.1 = ((f32[32,22,286]{2,1,0:T(8,128)}), f32[32,22,286]{2,1,0:T(8,128)S(1)}, u32[]{:S(2)}, u32[]{:S(2)}) async-start(f32[32,22,286]{2,1,0:T(8,128)} %pad_maximum_fusion), calls=%async_computation.1 | async-start | bytes 2359296 | tf_op jit(solution)/shard_map/all_to_all | solution.py:471
  40.2 13.1 %copy-start.4 = (s32[16,189]{1,0:T(8,128)S(1)}, s32[16,189]{1,0:T(8,128)}, u32[]{:S(2)}) copy-start(s32[16,189]{1,0:T(8,128)} %param.22) | copy-start | bytes 36292
  40.2 13.9 %copy-start.5 = (s32[16,189]{1,0:T(8,128)S(1)}, s32[16,189]{1,0:T(8,128)}, u32[]{:S(2)}) copy-start(s32[16,189]{1,0:T(8,128)} %param.23) | copy-start | bytes 36292
  119.8 1.0 copy-start.1

commit v4 on v3

--- a/solution.py
+++ b/solution.py
@@ -2,6 +2,7 @@
 
 import jax
 import jax.numpy as jnp
+import numpy as np
 from jax import lax
 from jax.experimental import pallas as pl
 from jax.experimental.pallas import tpu as pltpu
@@ -128,7 +129,7 @@
 
 
 def near_kernel(
-    leaves, width, count_ref, src_ref, off_ref, total_ref, data_ref, table_ref, out_ref,
+    leaves, count_ref, entry_ref, total_ref, data_ref, table_ref, out_ref,
     targets, acc, *held,
 ):
     bs, rs = held[:GROUP], held[GROUP:]
@@ -146,9 +147,7 @@
         square = jnp.sum(jnp.where(row < 3, t * t, 0.0), axis=0, keepdims=True)
         t = jnp.where(row < 3, -2.0 * t, jnp.where(row == 3, 1.0, jnp.where(row == 4, square, 0.0)))
         t1, t2, t3 = pieces(t)
-        zero = jnp.zeros((80, 128), f32)
-        full = jnp.concatenate([t1, t2, t3, t1, t2, t1, zero], axis=0)
-        targets[l] = full.T[:, :48].astype(bf16)
+        targets[l] = jnp.concatenate([t1, t2, t3, t1, t2, t1], axis=0).T.astype(bf16)
         acc[l] = jnp.zeros((128, 128), f32)
         return carry
 
@@ -157,9 +156,9 @@
     def build(l, k, b):
         named = []
         for j in range(QUAD):
-            entry = l * width + k + j
-            m = src_ref[entry]
-            s = data_ref[m] + table_ref[off_ref[entry]]
+            entry = entry_ref[l, k + j]
+            m = lax.shift_right_logical(entry, 5)
+            s = data_ref[m] + table_ref[lax.bitwise_and(entry, 31)]
             square = jnp.sum(jnp.where(row < 3, s * s, 0.0), axis=0, keepdims=True) + soft
             s = jnp.where(row == 3, square, s)
             s1, s2, s3 = pieces(s)
@@ -210,14 +209,14 @@
     lax.fori_loop(0, leaves // 8, finish, 0)
 
 
-def near_call(counts, sources, offsets, total, data, table, leaves, width):
+def near_call(counts, entries, total, data, table, leaves):
     vmem = pl.BlockSpec(memory_space=pltpu.VMEM)
     smem = pl.BlockSpec(memory_space=pltpu.SMEM)
     pairs = leaves * 18 * 128 * 128
     return pl.pallas_call(
-        functools.partial(near_kernel, leaves, width),
+        functools.partial(near_kernel, leaves),
         out_shape=jax.ShapeDtypeStruct((128, leaves), f32),
-        in_specs=[smem, smem, smem, smem, vmem, vmem],
+        in_specs=[smem, smem, smem, vmem, vmem],
         out_specs=vmem,
         scratch_shapes=[
             pltpu.VMEM((leaves, 128, 48), bf16),
@@ -228,7 +227,7 @@
         compiler_params=pltpu.CompilerParams(vmem_limit_bytes=VMEM_LIMIT),
         cost_estimate=pl.CostEstimate(flops=pairs * 96, bytes_accessed=1 << 20, transcendentals=pairs),
         name="near",
-    )(counts, sources, offsets, total, data, table)
+    )(counts, entries, total, data, table)
 
 
 def count_kernel(blocks, slot_ref, class_ref, out_ref, turned, high, low, held):
@@ -288,7 +287,7 @@
     o = pl.program_id(0)
     leaves, coef = own_ref.shape
     parents = pown_ref.shape[0]
-    coarse = coarse_src.shape[1]
+    coarse, across = coarse_src.shape[0], coarse_src.shape[1] // 2
     devices = got_ref.shape[0]
     cap_l, cap_p = caps
     operators = shifts.shape[0]
@@ -302,35 +301,36 @@
         total[...] = jnp.zeros_like(total)
         for copy in moves + copies:
             copy.start()
-        leaf_src[...] = jnp.zeros_like(leaf_src)
+        for source in (leaf_src, parent_src, coarse_src):
+            source[...] = jnp.zeros_like(source)
         parent_rows[...] = jnp.zeros_like(parent_rows)
         for side, half in enumerate(split2(own_ref[...])):
-            leaf_src[side, :leaves, :] = half
+            leaf_src[:leaves, side * across : side * across + coef] = half
         parent_rows[:parents, :] = pown_ref[...]
 
         for d in range(devices):
             got = got_ref[d]
             first, second = leaves + d * cap_l, parents + d * cap_p
             for side, half in enumerate(split2(got[:cap_l])):
-                leaf_src[side, first : first + cap_l, :] = half
+                leaf_src[first : first + cap_l, side * across : side * across + coef] = half
             parent_rows[second : second + cap_p, :] = got[cap_l : cap_l + cap_p]
             lifted_rows[d * grands : (d + 1) * grands, :] = got[cap_l + cap_p : cap_l + cap_p + grands]
         for side, half in enumerate(split2(parent_rows[...])):
-            parent_src[side] = half
+            parent_src[:, side * across : side * across + coef] = half
         sums = [jnp.sum(lifted_rows[8 * m : 8 * m + 8, :], axis=0, keepdims=True) for m in range(coarse)]
         for side, half in enumerate(split2(jnp.concatenate(sums, axis=0))):
-            coarse_src[side] = half
+            coarse_src[:, side * across : side * across + coef] = half
+
+    def added(lhs, source):
+        both = jnp.dot(lhs, source[...], preferred_element_type=f32)
+        return (both[:, :across] + both[:, across:])[:, :coef]
 
     def grouped(counts, source):
         lhs = jnp.concatenate([counts[0, b] for b in range(counts.shape[1])], axis=1)
-        return jnp.dot(lhs, source[0], preferred_element_type=f32) + jnp.dot(
-            lhs, source[1], preferred_element_type=f32
-        )
+        return added(lhs, source)
 
     few = cc_ref[0].astype(bf16)
-    small = jnp.dot(few, coarse_src[0], preferred_element_type=f32) + jnp.dot(
-        few, coarse_src[1], preferred_element_type=f32
-    )
+    small = added(few, coarse_src)
     stacked = jnp.concatenate([grouped(lc_ref, leaf_src), grouped(pc_ref, parent_src), small], axis=0)
     for i in range(operators):
 
@@ -405,9 +405,9 @@
         ],
         out_specs=vmem,
         scratch_shapes=[
-            pltpu.VMEM((2, lc.shape[1] * 128, coef), bf16),
-            pltpu.VMEM((2, pc.shape[1] * 128, coef), bf16),
-            pltpu.VMEM((2, ncoarse, coef), bf16),
+            pltpu.VMEM((lc.shape[1] * 128, 2 * wide), bf16),
+            pltpu.VMEM((pc.shape[1] * 128, 2 * wide), bf16),
+            pltpu.VMEM((ncoarse, 2 * wide), bf16),
             pltpu.VMEM((leaves + parents + ncoarse, coef), f32),
             pltpu.VMEM((wide // 128, leaves, 128), f32),
             pltpu.VMEM((wide // 128, parents, 128), f32),
@@ -475,14 +475,18 @@
     first = device * leaves
     padded = pl.cdiv(width, QUAD) * QUAD
     source = jnp.where(present, near_leaves - first + RIM, leaves + 2 * RIM)
-    source = jnp.pad(source, ((0, 1), (0, padded - width)), constant_values=leaves + 2 * RIM).reshape(-1)
-    offset = jnp.pad(jnp.where(present, near_offsets, 13), ((0, 1), (0, padded - width)), constant_values=13).reshape(-1)
+    entries = jnp.pad(
+        source * 32 + jnp.where(present, near_offsets, 13),
+        ((0, 1), (0, padded - width)),
+        constant_values=(leaves + 2 * RIM) * 32 + 13,
+    )
     counts = jnp.pad(jnp.sum(present.astype(jnp.int32), axis=1), (0, 1))
     total = jnp.sum((counts + QUAD - 1) // QUAD, keepdims=True)
-    classes = jnp.arange(27, dtype=jnp.int32)
-    shifts = jnp.stack([classes // 9 - 1, classes // 3 % 3 - 1, classes % 3 - 1], axis=1).astype(f32)
-    table = jnp.broadcast_to(jnp.pad(shifts, ((0, 0), (0, 5)))[:, :, None], (27, 8, size))
-    near = near_call(counts, source, offset, total, extended, table, leaves, padded)
+    classes = np.arange(27)
+    shifts = np.stack([classes // 9 - 1, classes // 3 % 3 - 1, classes % 3 - 1], axis=1)
+    table = np.zeros((27, 8, size), np.float32)
+    table[:, :3, :] = shifts[:, :, None]
+    near = near_call(counts, entries, total, extended, table, leaves)
     target_ids = first + jnp.arange(leaves, dtype=jnp.int32)
     alone = jnp.sum(
         ((near_leaves == target_ids[:, None]) & (near_offsets == 13)).astype(f32), axis=1

time: 148 us -> 147 us (level)
  local copies, waits for them, and re-layouts: 13.5 us -> 11.8 us
    unnamed x27 -> x26, local copies, waits for them, and re-layouts: 5.35 us -> 5.26 us
  transfers between devices with their start and end apart: 4 -> 4, of which waited for: 0 -> 0; matrix products, arithmetic and copies ran while one was open for 11% -> 10% of each run, Pallas kernels for 57% -> 58%
where the time goes in v4:
time: 147 us; the launch traced here: 145 us
  Pallas kernels  108 us (73%)
  starting transfers between devices  18.7 us (13%)
  local copies, waits for them, and re-layouts  11.8 us (8%)
  other arithmetic  5.12 us (3%)
    pallas_call x1, Pallas kernels, near_call(): pl.pallas_call(functools.partial(near_kernel, leaves), out_shape=jax.Shap...  59.8 us
    pallas_call x1, Pallas kernels, far_call(): pl.pallas_call(functools.partial(far_kernel, parents // 8, caps), grid=(o...  25.2 us
    pallas_call x2, Pallas kernels, count_call(): pl.pallas_call(functools.partial(count_kernel, blocks), out_shape=jax.Sha...  13.1 us
    pallas_call x1, Pallas kernels, upward_call(): pl.pallas_call(upward_kernel, out_shape=(jax.ShapeDtypeStruct((leaves, co...  10.4 us
    all_to_all x1, starting transfers between devices, per_device(): lax.all_to_all(outgoing, AXES, split_axis=0, concat_axis=0, tiled=True)  7.94 us
    all_to_all x1, starting transfers between devices, per_device(): lax.all_to_all(jnp.concatenate([leaf_plan, parent_plan], 2), AXES, split_...  7.3 us
    unnamed x26, local copies, waits for them, and re-layouts  5.26 us
  transfers between devices with their start and end apart: 4, of which 0 were waited for; matrix products, arithmetic and copies ran while one was open for 10% of the time, Pallas kernels for 58%

profile of v4, /device:TPU:0, one launch (start us, length us, event | category | flops | bytes accessed | tf_op | source)
XLA Modules:
  0.0 144.6 jit_solution(5400764164357824099)
XLA Ops:
  0.0 0.7 pad_add_fusion
  0.7 0.7 copy.67
  1.4 7.3 %all-to-all-start = ((s32[1,32,20]{2,0,1:T(1,128)}), s32[1,32,20]{2,0,1:T(1,128)S(1)}, u32[]{:S(2)}, u32[]{:S(2)}) async-start(s32[1,32,20]{2,0,1:T(1,128)} %copy.67), calls=%async_computation | async-start | bytes 32768 | tf_op jit(solution)/shard_map/all_to_all | solution.py:447
  8.7 1.6 %bitcast_dynamic-update-slice_fusion = (f32[128,8,128]{2,0,1:T(8,128)S(1)}, f32[3,128,128]{2,1,0:T(8,128)}) fusion(f32[1,3,128,128]{3,1,2,0:T(4,128)} %bitcast.34), kind=kLoop, calls=%fused_computation.6 | loop fusion | bytes 589824
  10.4 0.8 bitcast_dynamic-update-slice_fusion.1
  11.3 2.2 %collective-permute-start = (f32[32,8,128]{2,0,1:T(8,128)S(1)}, f32[32,8,128]{2,0,1:T(8,128)S(1)}, u32[]{:S(2)}, u32[]{:S(2)}) collective-permute-start(f32[32,8,128]{2,0,1:T(8,128)S(1)} %get-tuple-element.13), channel_id=1, source_target_pairs={{0,1},{1,2},{2,3},{3,4},{4,5},{5,6},{6,7},{7,8},{8,9},{9,10},{10,1... | collective-permute-start | bytes 393224 | tf_op jit(solution)/shard_map/ppermute | solution.py:458
  13.5 1.3 collective-permute-start.1
  14.8 0.1 copy.68
  14.9 0.1 copy.70
  15.0 0.1 select_add_fusion
  15.1 0.6 pad_add_fusion.1.ids_ref
  15.8 10.4 %upward.1 = (f32[128,286]{1,0:T(8,128)}, f32[16,286]{1,0:T(8,128)}, f32[2,286]{1,0:T(2,128)}) custom-call(s32[4]{0:T(128)} %pad_add_fusion.1.ids_ref, f32[3,128,128]{2,1,0:T(8,128)} %get-tuple-element.12.pos_ref, f32[128,128]{1,0:T(8,128)} %bitcast.29, f32[286,8,286]{2,1,0:T(8,128)} %bitcast.27), custom_call_target="tpu_custom_call" | custom-call | tf_op jit(solution)/shard_map/upward/pallas_call | solution.py:110
  26.3 0.1 reshape.49
  26.4 0.1 reshape.41
  26.5 1.6 %gather_fusion.1 = f32[128,286]{1,0:T(8,128)S(1)} fusion(f32[16,286]{1,0:T(8,128)} %get-tuple-element.9.pown_ref, s32[1024]{0:T(1024)S(1)} %get-tuple-element.21), kind=kCustom, calls=%fused_computation.1 | custom fusion | bytes 293376 | tf_op jit(solution)/shard_map/gather | solution.py:466
  28.2 1.6 %gather_fusion = f32[512,286]{1,0:T(8,128)S(1)} fusion(f32[128,286]{1,0:T(8,128)S(1)} %copy-done, s32[1024]{0:T(1024)S(1)} %get-tuple-element.22), kind=kCustom, calls=%fused_computation | custom fusion | bytes 1173504 | tf_op jit(solution)/shard_map/gather | solution.py:465
  29.9 1.1 pad_maximum_fusion
  31.0 7.9 %all-to-all-start.1 = ((f32[32,22,286]{2,1,0:T(8,128)}), f32[32,22,286]{2,1,0:T(8,128)S(1)}, u32[]{:S(2)}, u32[]{:S(2)}) async-start(f32[32,22,286]{2,1,0:T(8,128)} %pad_maximum_fusion), calls=%async_computation.1 | async-start | bytes 2359296 | tf_op jit(solution)/shard_map/all_to_all | solution.py:471
  39.0 1.2 fusion
  40.3 0.1 convert_reduce_fusion
  40.5 10.7 %count.2 = bf16[10240,128]{1,0:T(8,128)(2,1)} custom-call(s32[189,128]{1,0:T(8,128)} %bitcast.37, s32[189,128]{1,0:T(8,128)} %bitcast.38), custom_call_target="tpu_custom_call" | custom-call | flops 671088640 | bytes 2621440 | tf_op jit(solution)/shard_map/count/pallas_call | solution.py:261
  51.2 0.7 copy.75.cc_ref
  51.9 0.7 copy.65
  52.6 0.8 copy.66
  53.4 0.6 pad.9.entry_ref
  54.0 2.4 %count.3 = bf16[512,128]{1,0:T(8,128)(2,1)} custom-call(s32[189,16]{1,0:T(8,128)} %bitcast.32, s32[189,16]{1,0:T(8,128)} %bitcast.33), custom_call_target="tpu_custom_call" | custom-call | flops 33554432 | bytes 131072 | tf_op jit(solution)/shard_map/count/pallas_call | solution.py:261
  56.5 0.8 convert_reduce_fusion.2
  57.3 0.1 maximum_maximum_fusion
  57.4 1.0 copy.74.data_ref
  58.4 59.8 %near.1.near_ref = f32[128,128]{1,0:T(8,128)} custom-call(s32[129]{0:T(256)} %get-tuple-element.18.count_ref, s32[129,28]{1,0:T(8,128)} %pad.9.entry_ref, s32[1]{0:T(128)} %bitcast.13.total_ref, f32[193,8,128]{2,1,0:T(8,128)} %copy.74.data_ref, f32[27,8,128]{2,1,0:T(8,128)} %constant.81.clone.table_ref), custom_call_target="tpu_custom_call" | custom-call | flops 3623878656 | bytes 1048576 | tf_op jit(solution)/shard_map/near/pallas_call | solution.py:216
  118.2 1.0 copy-done.1
  119.2 25.2 %far.1 = f32[128,128]{1,0:T(8,128)} custom-call(s32[4]{0:T(128)} %pad_add_fusion.1.ids_ref, bf16[16,5,128,128]{3,2,1,0:T(8,128)(2,1)} %bitcast.24, bf16[16,2,16,128]{3,2,1,0:T(8,128)(2,1)} %bitcast.31, f32[16,8,8]{2,1,0:T(8,128)} %copy.75.cc_ref, f32[128,286]{1,0:T(8,128)} %get-tuple-element.8.own_ref, f32[16,286]{1,0:T(8,128)} %get-tuple-element.9.pown_ref, ...), custom_call_target="tpu_custom_call" | custom-call | tf_op jit(solution)/shard_map/far/pallas_call | solution.py:398
  (36 shorter events, 0.5 us)
Async XLA Ops:
  0.0 14.8 %copy-start.2 = (s32[128,27]{0,1:T(8,128)S(1)}, s32[128,27]{0,1:T(8,128)}, u32[]{:S(2)}) copy-start(s32[128,27]{0,1:T(8,128)} %param.18) | copy-start | bytes 41476
  0.0 14.9 %copy-start.3 = (s32[128,27]{0,1:T(8,128)S(1)}, s32[128,27]{0,1:T(8,128)}, u32[]{:S(2)}) copy-start(s32[128,27]{0,1:T(8,128)} %param.19) | copy-start | bytes 41476
  1.4 24.8 %all-to-all-start = ((s32[1,32,20]{2,0,1:T(1,128)}), s32[1,32,20]{2,0,1:T(1,128)S(1)}, u32[]{:S(2)}, u32[]{:S(2)}) async-start(s32[1,32,20]{2,0,1:T(1,128)} %copy.67), calls=%async_computation | async-start | bytes 32768 | tf_op jit(solution)/shard_map/all_to_all | solution.py:447
  11.3 46.0 %collective-permute-start = (f32[32,8,128]{2,0,1:T(8,128)S(1)}, f32[32,8,128]{2,0,1:T(8,128)S(1)}, u32[]{:S(2)}, u32[]{:S(2)}) collective-permute-start(f32[32,8,128]{2,0,1:T(8,128)S(1)} %get-tuple-element.13), channel_id=1, source_target_pairs={{0,1},{1,2},{2,3},{3,4},{4,5},{5,6},{6,7},{7,8},{8,9},{9,10},{10,1... | collective-permute-start | bytes 393224 | tf_op jit(solution)/shard_map/ppermute | solution.py:458
  13.5 43.8 %collective-permute-start.1 = (f32[32,8,128]{2,0,1:T(8,128)S(1)}, f32[32,8,128]{2,0,1:T(8,128)S(1)}, u32[]{:S(2)}, u32[]{:S(2)}) collective-permute-start(f32[32,8,128]{2,0,1:T(8,128)S(1)} %get-tuple-element.14), channel_id=1, source_target_pairs={{1,0},{2,1},{3,2},{4,3},{5,4},{6,5},{7,6},{8,7},{9,8},{10,9},{11,1... | collective-permute-start | bytes 393224 | tf_op jit(solution)/shard_map/ppermute | solution.py:459
  26.2 2.0 %copy-start = (f32[128,286]{1,0:T(8,128)S(1)}, f32[128,286]{1,0:T(8,128)}, u32[]{:S(2)}) copy-start(f32[128,286]{1,0:T(8,128)} %get-tuple-element.8.own_ref) | copy-start | bytes 439300
  28.2 1.6 %copy-start.8 = (f32[2,286]{1,0:T(2,128)S(1)}, f32[2,286]{1,0:T(2,128)}, u32[]{:S(2)}) copy-start(f32[2,286]{1,0:T(2,128)} %get-tuple-element.10) | copy-start | bytes 6868
  31.0 9.2 %copy-start.6 = (s32[8,7]{1,0:T(8,128)S(1)}, s32[8,7]{1,0:T(8,128)}, u32[]{:S(2)}) copy-start(s32[8,7]{1,0:T(8,128)} %param.26) | copy-start | bytes 676
  31.0 9.2 %copy-start.7 = (s32[8,7]{1,0:T(8,128)S(1)}, s32[8,7]{1,0:T(8,128)}, u32[]{:S(2)}) copy-start(s32[8,7]{1,0:T(8,128)} %param.27) | copy-start | bytes 676
  31.0 87.2 %all-to-all-start.1 = ((f32[32,22,286]{2,1,0:T(8,128)}), f32[32,22,286]{2,1,0:T(8,128)S(1)}, u32[]{:S(2)}, u32[]{:S(2)}) async-start(f32[32,22,286]{2,1,0:T(8,128)} %pad_maximum_fusion), calls=%async_computation.1 | async-start | bytes 2359296 | tf_op jit(solution)/shard_map/all_to_all | solution.py:471
  40.5 11.4 %copy-start.4 = (s32[16,189]{1,0:T(8,128)S(1)}, s32[16,189]{1,0:T(8,128)}, u32[]{:S(2)}) copy-start(s32[16,189]{1,0:T(8,128)} %param.23) | copy-start | bytes 36292
  40.5 12.1 %copy-start.5 = (s32[16,189]{1,0:T(8,128)S(1)}, s32[16,189]{1,0:T(8,128)}, u32[]{:S(2)}) copy-start(s32[16,189]{1,0:T(8,128)} %param.24) | copy-start | bytes 36292
  118.2 1.0 copy-start.1

commit v5 on v4

--- a/solution.py
+++ b/solution.py
@@ -11,7 +11,7 @@
 ORDER = 10
 RIM = 32
 QUAD = 4
-GROUP = 4
+GROUP = 8
 softening = 0.05
 AXES = ("gx", "gy")
 VMEM_LIMIT = 56 * 1024 * 1024

time: 147 us -> 141 us (0.959)
  the two profiles are of different devices: /device:TPU:0 before, /device:TPU:1 now
where the time goes in v5:
time: 141 us
  Pallas kernels  105 us (74%)
  starting transfers between devices  18.5 us (13%)
  local copies, waits for them, and re-layouts  11.8 us (8%)
  other arithmetic  5.12 us (4%)
    pallas_call x1, Pallas kernels, near_call(): pl.pallas_call(functools.partial(near_kernel, leaves), out_shape=jax.Shap...  56.5 us
    pallas_call x1, Pallas kernels, far_call(): pl.pallas_call(functools.partial(far_kernel, parents // 8, caps), grid=(o...  25.2 us
    pallas_call x2, Pallas kernels, count_call(): pl.pallas_call(functools.partial(count_kernel, blocks), out_shape=jax.Sha...  13.1 us
    pallas_call x1, Pallas kernels, upward_call(): pl.pallas_call(upward_kernel, out_shape=(jax.ShapeDtypeStruct((leaves, co...  10.4 us
    all_to_all x1, starting transfers between devices, per_device(): lax.all_to_all(jnp.concatenate([leaf_plan, parent_plan], 2), AXES, split_...  7.1 us
    all_to_all x1, starting transfers between devices, per_device(): lax.all_to_all(outgoing, AXES, split_axis=0, concat_axis=0, tiled=True)  5.93 us
    unnamed x26, local copies, waits for them, and re-layouts  5.26 us
    ppermute x1, starting transfers between devices, per_device(): before = lax.ppermute(data[leaves - RIM:], AXES, up)  3.54 us
  transfers between devices with their start and end apart: 4, of which 0 were waited for; matrix products, arithmetic and copies ran while one was open for 10% of the time, Pallas kernels for 57%

profile of v5, /device:TPU:1, one launch (start us, length us, event | category | flops | bytes accessed | tf_op | source)
XLA Modules:
  0.0 141.1 jit_solution(7594065864291267355)
XLA Ops:
  0.0 0.7 pad_add_fusion
  0.7 0.7 copy.67
  1.4 7.1 %all-to-all-start = ((s32[1,32,20]{2,0,1:T(1,128)}), s32[1,32,20]{2,0,1:T(1,128)S(1)}, u32[]{:S(2)}, u32[]{:S(2)}) async-start(s32[1,32,20]{2,0,1:T(1,128)} %copy.67), calls=%async_computation | async-start | bytes 32768 | tf_op jit(solution)/shard_map/all_to_all | solution.py:447
  8.5 1.6 %bitcast_dynamic-update-slice_fusion = (f32[128,8,128]{2,0,1:T(8,128)S(1)}, f32[3,128,128]{2,1,0:T(8,128)}) fusion(f32[1,3,128,128]{3,1,2,0:T(4,128)} %bitcast.34), kind=kLoop, calls=%fused_computation.6 | loop fusion | bytes 589824
  10.2 0.8 bitcast_dynamic-update-slice_fusion.1
  11.1 3.5 %collective-permute-start = (f32[32,8,128]{2,0,1:T(8,128)S(1)}, f32[32,8,128]{2,0,1:T(8,128)S(1)}, u32[]{:S(2)}, u32[]{:S(2)}) collective-permute-start(f32[32,8,128]{2,0,1:T(8,128)S(1)} %get-tuple-element.13), channel_id=1, source_target_pairs={{0,1},{1,2},{2,3},{3,4},{4,5},{5,6},{6,7},{7,8},{8,9},{9,10},{10,1... | collective-permute-start | bytes 393224 | tf_op jit(solution)/shard_map/ppermute | solution.py:458
  14.6 1.9 %collective-permute-start.1 = (f32[32,8,128]{2,0,1:T(8,128)S(1)}, f32[32,8,128]{2,0,1:T(8,128)S(1)}, u32[]{:S(2)}, u32[]{:S(2)}) collective-permute-start(f32[32,8,128]{2,0,1:T(8,128)S(1)} %get-tuple-element.14), channel_id=1, source_target_pairs={{1,0},{2,1},{3,2},{4,3},{5,4},{6,5},{7,6},{8,7},{9,8},{10,9},{11,1... | collective-permute-start | bytes 393224 | tf_op jit(solution)/shard_map/ppermute | solution.py:459
  16.6 0.1 copy.68
  16.7 0.1 copy.70
  16.8 0.1 select_add_fusion
  16.9 0.6 pad_add_fusion.1.ids_ref
  17.6 10.4 %upward.1 = (f32[128,286]{1,0:T(8,128)}, f32[16,286]{1,0:T(8,128)}, f32[2,286]{1,0:T(2,128)}) custom-call(s32[4]{0:T(128)} %pad_add_fusion.1.ids_ref, f32[3,128,128]{2,1,0:T(8,128)} %get-tuple-element.12.pos_ref, f32[128,128]{1,0:T(8,128)} %bitcast.29, f32[286,8,286]{2,1,0:T(8,128)} %bitcast.27), custom_call_target="tpu_custom_call" | custom-call | tf_op jit(solution)/shard_map/upward/pallas_call | solution.py:110
  28.1 0.1 reshape.49
  28.2 0.1 reshape.41
  28.3 1.6 %gather_fusion.1 = f32[128,286]{1,0:T(8,128)S(1)} fusion(f32[16,286]{1,0:T(8,128)} %get-tuple-element.9.pown_ref, s32[1024]{0:T(1024)S(1)} %get-tuple-element.21), kind=kCustom, calls=%fused_computation.1 | custom fusion | bytes 293376 | tf_op jit(solution)/shard_map/gather | solution.py:466
  30.0 1.6 %gather_fusion = f32[512,286]{1,0:T(8,128)S(1)} fusion(f32[128,286]{1,0:T(8,128)S(1)} %copy-done, s32[1024]{0:T(1024)S(1)} %get-tuple-element.22), kind=kCustom, calls=%fused_computation | custom fusion | bytes 1173504 | tf_op jit(solution)/shard_map/gather | solution.py:465
  31.7 1.1 pad_maximum_fusion
  32.8 5.9 %all-to-all-start.1 = ((f32[32,22,286]{2,1,0:T(8,128)}), f32[32,22,286]{2,1,0:T(8,128)S(1)}, u32[]{:S(2)}, u32[]{:S(2)}) async-start(f32[32,22,286]{2,1,0:T(8,128)} %pad_maximum_fusion), calls=%async_computation.1 | async-start | bytes 2359296 | tf_op jit(solution)/shard_map/all_to_all | solution.py:471
  38.8 1.2 fusion
  40.1 0.1 convert_reduce_fusion
  40.3 10.7 %count.2 = bf16[10240,128]{1,0:T(8,128)(2,1)} custom-call(s32[189,128]{1,0:T(8,128)} %bitcast.37, s32[189,128]{1,0:T(8,128)} %bitcast.38), custom_call_target="tpu_custom_call" | custom-call | flops 671088640 | bytes 2621440 | tf_op jit(solution)/shard_map/count/pallas_call | solution.py:261
  51.0 0.7 copy.75.cc_ref
  51.7 0.7 copy.65
  52.4 0.8 copy.66
  53.2 0.6 pad.9.entry_ref
  53.8 2.4 %count.3 = bf16[512,128]{1,0:T(8,128)(2,1)} custom-call(s32[189,16]{1,0:T(8,128)} %bitcast.32, s32[189,16]{1,0:T(8,128)} %bitcast.33), custom_call_target="tpu_custom_call" | custom-call | flops 33554432 | bytes 131072 | tf_op jit(solution)/shard_map/count/pallas_call | solution.py:261
  56.3 0.8 convert_reduce_fusion.2
  57.1 0.1 maximum_maximum_fusion
  57.2 1.0 copy.74.data_ref
  58.2 56.5 %near.1.near_ref = f32[128,128]{1,0:T(8,128)} custom-call(s32[129]{0:T(256)} %get-tuple-element.18.count_ref, s32[129,28]{1,0:T(8,128)} %pad.9.entry_ref, s32[1]{0:T(128)} %bitcast.13.total_ref, f32[193,8,128]{2,1,0:T(8,128)} %copy.74.data_ref, f32[27,8,128]{2,1,0:T(8,128)} %constant.81.clone.table_ref), custom_call_target="tpu_custom_call" | custom-call | flops 3623878656 | bytes 1048576 | tf_op jit(solution)/shard_map/near/pallas_call | solution.py:216
  114.8 1.0 copy-done.1
  115.8 25.2 %far.1 = f32[128,128]{1,0:T(8,128)} custom-call(s32[4]{0:T(128)} %pad_add_fusion.1.ids_ref, bf16[16,5,128,128]{3,2,1,0:T(8,128)(2,1)} %bitcast.24, bf16[16,2,16,128]{3,2,1,0:T(8,128)(2,1)} %bitcast.31, f32[16,8,8]{2,1,0:T(8,128)} %copy.75.cc_ref, f32[128,286]{1,0:T(8,128)} %get-tuple-element.8.own_ref, f32[16,286]{1,0:T(8,128)} %get-tuple-element.9.pown_ref, ...), custom_call_target="tpu_custom_call" | custom-call | tf_op jit(solution)/shard_map/far/pallas_call | solution.py:398
  (36 shorter events, 0.5 us)
Async XLA Ops:
  0.0 16.6 %copy-start.2 = (s32[128,27]{0,1:T(8,128)S(1)}, s32[128,27]{0,1:T(8,128)}, u32[]{:S(2)}) copy-start(s32[128,27]{0,1:T(8,128)} %param.18) | copy-start | bytes 41476
  0.0 16.7 %copy-start.3 = (s32[128,27]{0,1:T(8,128)S(1)}, s32[128,27]{0,1:T(8,128)}, u32[]{:S(2)}) copy-start(s32[128,27]{0,1:T(8,128)} %param.19) | copy-start | bytes 41476
  1.4 26.6 %all-to-all-start = ((s32[1,32,20]{2,0,1:T(1,128)}), s32[1,32,20]{2,0,1:T(1,128)S(1)}, u32[]{:S(2)}, u32[]{:S(2)}) async-start(s32[1,32,20]{2,0,1:T(1,128)} %copy.67), calls=%async_computation | async-start | bytes 32768 | tf_op jit(solution)/shard_map/all_to_all | solution.py:447
  11.1 46.0 %collective-permute-start = (f32[32,8,128]{2,0,1:T(8,128)S(1)}, f32[32,8,128]{2,0,1:T(8,128)S(1)}, u32[]{:S(2)}, u32[]{:S(2)}) collective-permute-start(f32[32,8,128]{2,0,1:T(8,128)S(1)} %get-tuple-element.13), channel_id=1, source_target_pairs={{0,1},{1,2},{2,3},{3,4},{4,5},{5,6},{6,7},{7,8},{8,9},{9,10},{10,1... | collective-permute-start | bytes 393224 | tf_op jit(solution)/shard_map/ppermute | solution.py:458
  14.6 42.4 %collective-permute-start.1 = (f32[32,8,128]{2,0,1:T(8,128)S(1)}, f32[32,8,128]{2,0,1:T(8,128)S(1)}, u32[]{:S(2)}, u32[]{:S(2)}) collective-permute-start(f32[32,8,128]{2,0,1:T(8,128)S(1)} %get-tuple-element.14), channel_id=1, source_target_pairs={{1,0},{2,1},{3,2},{4,3},{5,4},{6,5},{7,6},{8,7},{9,8},{10,9},{11,1... | collective-permute-start | bytes 393224 | tf_op jit(solution)/shard_map/ppermute | solution.py:459
  28.0 2.0 %copy-start = (f32[128,286]{1,0:T(8,128)S(1)}, f32[128,286]{1,0:T(8,128)}, u32[]{:S(2)}) copy-start(f32[128,286]{1,0:T(8,128)} %get-tuple-element.8.own_ref) | copy-start | bytes 439300
  30.0 1.6 %copy-start.8 = (f32[2,286]{1,0:T(2,128)S(1)}, f32[2,286]{1,0:T(2,128)}, u32[]{:S(2)}) copy-start(f32[2,286]{1,0:T(2,128)} %get-tuple-element.10) | copy-start | bytes 6868
  32.8 7.2 %copy-start.6 = (s32[8,7]{1,0:T(8,128)S(1)}, s32[8,7]{1,0:T(8,128)}, u32[]{:S(2)}) copy-start(s32[8,7]{1,0:T(8,128)} %param.26) | copy-start | bytes 676
  32.8 7.2 %copy-start.7 = (s32[8,7]{1,0:T(8,128)S(1)}, s32[8,7]{1,0:T(8,128)}, u32[]{:S(2)}) copy-start(s32[8,7]{1,0:T(8,128)} %param.27) | copy-start | bytes 676
  32.8 82.0 %all-to-all-start.1 = ((f32[32,22,286]{2,1,0:T(8,128)}), f32[32,22,286]{2,1,0:T(8,128)S(1)}, u32[]{:S(2)}, u32[]{:S(2)}) async-start(f32[32,22,286]{2,1,0:T(8,128)} %pad_maximum_fusion), calls=%async_computation.1 | async-start | bytes 2359296 | tf_op jit(solution)/shard_map/all_to_all | solution.py:471
  40.3 11.4 %copy-start.4 = (s32[16,189]{1,0:T(8,128)S(1)}, s32[16,189]{1,0:T(8,128)}, u32[]{:S(2)}) copy-start(s32[16,189]{1,0:T(8,128)} %param.23) | copy-start | bytes 36292
  40.3 12.1 %copy-start.5 = (s32[16,189]{1,0:T(8,128)S(1)}, s32[16,189]{1,0:T(8,128)}, u32[]{:S(2)}) copy-start(s32[16,189]{1,0:T(8,128)} %param.24) | copy-start | bytes 36292
  114.8 1.0 copy-start.1
